TPU v7x, 32 devices: a whole 2x2x4 slice. The times are simulated.
32 devices in a mesh: rep: 2 (over y), pipe: 8 (over z, x), tp: 2 (over core).
Axes of the slice: x: 2, y: 2, z: 4, core: 2. Of those that a mesh axis runs over, the one named last changes fastest.
Arguments:
- act_forward: bfloat16 [8, 2, 128, 4096], P('pipe', 'rep', 'tp'), may hold values from -6 to 6
- act_saved: bfloat16 [8, 2, 128, 4096], P('pipe', 'rep', 'tp'), may hold values from -6 to 6
- grad_output: bfloat16 [8, 2, 128, 4096], P('pipe', 'rep', 'tp'), may hold values from -6 to 6
- norm_gain: bfloat16 [8, 4096], P('pipe'), may hold values from 0.099609375 to 1.8984375
- up_weight: bfloat16 [8, 4096, 14336], P('pipe', None, ('rep', 'tp')), may hold values from -0.09375 to 0.09375
- down_weight: bfloat16 [8, 14336, 4096], P('pipe', ('rep', 'tp')), may hold values from -0.046875 to 0.046875
- section_layers: int32 [4], replicated, may hold values from 1 to 3, 8 in all
- redirect_count: int32 [3, 2], replicated, may hold values from 0 to 3, as said below
- redirect_dest: int32 [3, 2], replicated, may hold values from 0 to 1, as said below
Outputs:
- arrive_forward: bfloat16 [8, 2, 128, 4096], P('pipe', 'rep', 'tp')
- arrive_backward: bfloat16 [8, 2, 128, 4096], P('pipe', 'rep', 'tp')
Inputs may be any that keep to these rules, and one draw needn't show every extreme that they name: `redirect_count`: counts are in blocks of 16 rows. At each boundary every replica either sends to another replica or has count zero; a sender's destination has count zero there, and each replica receives from at most one sender. Following the boundaries in order from 5 live blocks, every replica keeps at least one block and never holds more than 8. At the first boundary every sender sends to the replica 2 / 2 indices away (counted round); one replica sends exactly 3 blocks, filling its receiver to 8, and with four or more replicas another replica sends exactly one block. `redirect_dest`: the destination of a replica with count zero is the replica itself.
All inputs are finite; a program needn't handle non-finite values.
Results may differ from a plain program's by a relative error of at most 0.015.
Values may be sent and summed in bfloat16 or wider, within the bound.
A program may use at most 128 MiB of HBM per device.

v0:
```python
import jax
import jax.numpy as jnp
from jax import lax
from jax.sharding import PartitionSpec as P

BLOCK = 16
CAPB = 8
START = 5


EPSILON = 1e-05


def from_behind(block, axis, distance):
    devices = range(lax.axis_size(axis))
    route = [(i - distance, i) for i in devices if i - distance in devices]
    return lax.ppermute(block, axis, route)


def moved_blocks(counts, dests, replica_ids):
    return jnp.where((dests != replica_ids) & (counts > 0), counts, 0)


def section_plan(section_layers, redirect_count, redirect_dest, segments, replicas):
    replica_ids = jnp.arange(replicas, dtype=jnp.int32)
    section_ends = (jnp.cumsum(section_layers) - 1)[:-1]
    positions = jnp.arange(segments, dtype=jnp.int32)
    matches = (section_ends[None, :] == positions[:, None]).astype(jnp.int32)
    segment_count = jnp.sum(matches[:, :, None] * redirect_count[None, :, :], axis=1)
    has_boundary = jnp.sum(matches, axis=1)[:, None]
    segment_dest = (
        jnp.sum(matches[:, :, None] * redirect_dest[None, :, :], axis=1)
        + (1 - has_boundary) * replica_ids[None, :]
    )
    live_list = [jnp.full((replicas,), START, jnp.int32)]
    for position in range(segments - 1):
        moved = moved_blocks(segment_count[position], segment_dest[position], replica_ids)
        incoming = jnp.sum(
            jnp.where(segment_dest[position][:, None] == replica_ids[None, :], moved[:, None], 0),
            axis=0,
        )
        live_list.append(live_list[-1] - moved + incoming)
    return (jnp.stack(live_list), segment_count, segment_dest)


def source_rows(live_before, counts, dests, replicas):
    replica_ids = jnp.arange(replicas, dtype=jnp.int32)
    block_ids = jnp.arange(CAPB, dtype=jnp.int32)
    moved = moved_blocks(counts, dests, replica_ids)
    sends = moved > 0
    same_dest = (
        (dests[None, :] == dests[:, None])
        & (replica_ids[None, :] < replica_ids[:, None])
        & sends[None, :]
    )
    kept = live_before - moved
    incoming = jnp.sum(
        jnp.where(sends[:, None] & (dests[:, None] == replica_ids[None, :]), moved[:, None], 0),
        axis=0,
    )
    offset = jnp.sum(jnp.where(same_dest, moved[None, :], 0), axis=1)
    hits = (
        sends[None, None, :]
        & (dests[None, None, :] == replica_ids[:, None, None])
        & (block_ids[None, :, None] >= offset[None, None, :])
        & (block_ids[None, :, None] < (offset + moved)[None, None, :])
    )
    from_block = (
        replica_ids[None, None, :] * CAPB + block_ids[None, :, None] - offset[None, None, :]
    )
    moved_source = jnp.sum(jnp.where(hits, from_block, 0), axis=2)
    own_local = block_ids[None, :] - incoming[:, None]
    own_ok = (own_local >= 0) & (own_local < kept[:, None])
    own_block = own_local + moved[:, None]
    source_block = jnp.where(
        jnp.any(hits, axis=2),
        moved_source,
        jnp.where(own_ok, replica_ids[:, None] * CAPB + own_block, -1),
    )
    row_ids = source_block[:, :, None] * BLOCK + jnp.arange(BLOCK, dtype=jnp.int32)[None, None, :]
    return jnp.where(source_block[:, :, None] >= 0, row_ids, -1).reshape(replicas * CAPB * BLOCK)


def inverse_rows(source):
    total = source.shape[0]
    target = jnp.where(source >= 0, source, total)
    return (
        jnp.full((total,), -1, jnp.int32)
        .at[target]
        .set(jnp.arange(total, dtype=jnp.int32), mode="drop")
    )


def pick_rows(values, index):
    taken = jnp.take(values, jnp.maximum(index, 0), axis=0)
    return jnp.where(index[:, None] >= 0, taken, jnp.zeros((), values.dtype))


def normalize(values, gain_row):
    wide = values.astype(jnp.float32)
    scale = lax.rsqrt(jnp.mean(wide * wide, axis=-1, keepdims=True) + EPSILON)
    return (wide * scale * gain_row.astype(jnp.float32)).astype(jnp.bfloat16)


def norm_back(values, gain_row, upstream):
    wide = values.astype(jnp.float32)
    scale = lax.rsqrt(jnp.mean(wide * wide, axis=-1, keepdims=True) + EPSILON)
    weighted = gain_row.astype(jnp.float32) * upstream
    return scale * weighted - wide * (scale * scale * scale) * jnp.mean(
        weighted * wide, axis=-1, keepdims=True
    )


def silu_slope(upper):
    sigma = jax.nn.sigmoid(upper)
    return sigma * (1.0 + upper * (1.0 - sigma))


def against_rows(left, right):
    return lax.dot_general(
        left, right, (((1,), (1,)), ((), ())), preferred_element_type=jnp.float32
    )


def route_rows(own_result, own_grad, later_mine, earlier_mine):
    every_result, every_grad = (
        lax.all_gather(own_result, ("rep", "tp"), axis=0, tiled=True),
        lax.all_gather(own_grad, ("rep", "tp"), axis=0, tiled=True),
    )
    return (pick_rows(every_result, later_mine), pick_rows(every_grad, earlier_mine))


def local(
    act_forward,
    act_saved,
    grad_output,
    norm_gain,
    up_weight,
    down_weight,
    section_layers,
    redirect_count,
    redirect_dest,
):
    segments = lax.axis_size("pipe")
    replicas = lax.axis_size("rep")
    splits = lax.axis_size("tp")
    segment_index = lax.axis_index("pipe")
    replica_index = lax.axis_index("rep")
    split_index = lax.axis_index("tp")
    fresh_own = act_forward[0, 0]
    saved_own = act_saved[0, 0]
    upstream_own = grad_output[0, 0]
    local_rows = fresh_own.shape[0]
    gain_row = norm_gain[0]
    w_up = up_weight[0]
    w_down = down_weight[0]
    live, segment_count, segment_dest = section_plan(
        section_layers, redirect_count, redirect_dest, segments, replicas
    )
    prior = jnp.maximum(segment_index - 1, 0)
    later = source_rows(
        live[segment_index], segment_count[segment_index], segment_dest[segment_index], replicas
    )
    earlier = inverse_rows(
        source_rows(live[prior], segment_count[prior], segment_dest[prior], replicas)
    )
    my_offset = (replica_index * splits + split_index) * local_rows
    later_mine = lax.dynamic_slice_in_dim(later, my_offset, local_rows)
    earlier_mine = lax.dynamic_slice_in_dim(earlier, my_offset, local_rows)
    fresh, saved, upstream = (
        lax.all_gather(fresh_own, ("rep", "tp"), axis=0, tiled=True),
        lax.all_gather(saved_own, ("rep", "tp"), axis=0, tiled=True),
        lax.all_gather(upstream_own, ("rep", "tp"), axis=0, tiled=True),
    )
    hidden = jax.nn.silu(
        jnp.dot(normalize(fresh, gain_row), w_up, preferred_element_type=jnp.float32)
    ).astype(jnp.bfloat16)
    upper = jnp.dot(normalize(saved, gain_row), w_up, preferred_element_type=jnp.float32)
    back_hidden = (against_rows(upstream, w_down) * silu_slope(upper)).astype(jnp.bfloat16)
    mixed = lax.psum_scatter(
        jnp.dot(hidden, w_down, preferred_element_type=jnp.float32).astype(jnp.bfloat16),
        ("rep", "tp"),
        scatter_dimension=0,
        tiled=True,
    ).astype(jnp.float32)
    returned = lax.psum_scatter(
        against_rows(back_hidden, w_up).astype(jnp.bfloat16),
        ("rep", "tp"),
        scatter_dimension=0,
        tiled=True,
    ).astype(jnp.float32)
    own_result = (fresh_own.astype(jnp.float32) + mixed).astype(jnp.bfloat16)
    own_grad = (upstream_own.astype(jnp.float32) + norm_back(saved_own, gain_row, returned)).astype(
        jnp.bfloat16
    )
    result, gradient = route_rows(own_result, own_grad, later_mine, earlier_mine)
    arrive_forward = from_behind(result, "pipe", 1)
    arrive_backward = from_behind(gradient, "pipe", -1)
    return (arrive_forward[None, None], arrive_backward[None, None])


def solution(mesh):
    in_specs = (
        P("pipe", "rep", "tp", None),
        P("pipe", "rep", "tp", None),
        P("pipe", "rep", "tp", None),
        P("pipe", None),
        P("pipe", None, ("rep", "tp")),
        P("pipe", ("rep", "tp"), None),
        P(),
        P(),
        P(),
    )
    out_specs = (P("pipe", "rep", "tp", None), P("pipe", "rep", "tp", None))
    return jax.shard_map(local, mesh=mesh, in_specs=in_specs, out_specs=out_specs, check_vma=False)
```

profile of v0, /device:TPU:8, one launch (start us, length us, event | category | flops | bytes accessed | tf_op | source)
XLA Modules:
  0.0 231.9 jit_solution(15394083541702100800)
XLA Ops:
  9.4 0.8 reduce-window.9
  10.4 0.8 copy.42
  11.2 0.8 copy.43
  13.5 19.9 %all-gather.17.cloned.1.call-done = bf16[1,1,256,4096]{3,2,1,0:T(8,128)(2,1)} async-done(((bf16[1,1,64,4096]{3,2,1,0:T(8,128)(2,1)}), bf16[1,1,256,4096]{3,2,1,0:T(8,128)(2,1)}) %all-gather.17.cloned.1.call-update) | async-done | bytes 2097168 | tf_op jit(solution)/shard_map/all_gather | solution.py:172
  33.3 2.1 fusion.25
  35.4 15.9 %fusion.6 = f32[256,3584]{1,0:T(8,128)} fusion(bf16[1,4096,3584]{2,1,0:T(8,128)(2,1)} %param.15, bf16[1,1,256,4096]{3,2,1,0:T(8,128)(2,1)} %all-gather.17.cloned.1.call-done, f32[256]{0:T(256)S(1)} %add_rsqrt_fusion, f32[4096]{0:T(1024)S(1)} %bitcast.73), kind=kOutput, calls=%fused_computation.9 | convolution fusion | flops 7520387072 | bytes 35144704 | tf_op jit(solution)/shard_map/dot_general | solution.py:178
  51.4 6.2 %all-gather.15.cloned.1.call-done = bf16[1,1,256,4096]{3,2,1,0:T(8,128)(2,1)} async-done(((bf16[1,1,64,4096]{3,2,1,0:T(8,128)(2,1)}), bf16[1,1,256,4096]{3,2,1,0:T(8,128)(2,1)}) %all-gather.15.cloned.1.call-update) | async-done | bytes 2097168 | tf_op jit(solution)/shard_map/all_gather | solution.py:173
  57.5 30.4 %fusion.13 = bf16[256,4096]{1,0:T(8,128)(2,1)} fusion(bf16[1,4096,3584]{2,1,0:T(8,128)(2,1)} %param.15, bf16[1,3584,4096]{2,1,0:T(8,128)(2,1)} %param.16, f32[256,3584]{1,0:T(8,128)} %fusion.6, bf16[1,1,256,4096]{3,2,1,0:T(8,128)(2,1)} %all-gather.15.cloned.1.call-done), kind=kOutput, calls=%fused_computation.18 | convolution fusion | flops 15041691648 | bytes 66584576 | tf_op jit(solution)/shard_map/dot_general | solution.py:120
  88.2 2.1 fusion.22
  90.3 30.8 %fusion.19 = bf16[256,4096]{1,0:T(8,128)(2,1)} fusion(bf16[1,3584,4096]{2,1,0:T(8,128)(2,1)} %param.16, bf16[1,4096,3584]{2,1,0:T(8,128)(2,1)} %param.15, bf16[1,1,256,4096]{3,2,1,0:T(8,128)(2,1)} %all-gather.13.cloned.1.call-done, f32[4096]{0:T(1024)S(1)} %bitcast.74, f32[256]{0:T(256)S(1)} %add_rsqrt_fusion.1), kind=kOutput, calls=%fused_computation.20 | convolution fusion | flops 15042215936 | bytes 62931968 | tf_op jit(solution)/shard_map/dot_general | solution.py:181
  123.0 1.4 fusion.53
  124.4 2.2 fusion.57
  128.0 25.9 %reduce-scatter.3.cloned.1.call-done = bf16[64,4096]{1,0:T(8,128)(2,1)} async-done(((bf16[256,4096]{1,0:T(8,128)(2,1)}), bf16[64,4096]{1,0:T(8,128)(2,1)}) %reduce-scatter.3.cloned.1.call-update) | async-done | bytes 524304 | tf_op jit(solution)/shard_map/reduce_scatter | solution.py:180
  153.9 2.0 fusion.59
  156.5 1.4 scatter_custom_fusion
  158.1 20.4 %all-gather.11.cloned.1.call-done = bf16[256,4096]{1,0:T(8,128)(2,1)} async-done(((bf16[64,4096]{1,0:T(8,128)(2,1)}), bf16[256,4096]{1,0:T(8,128)(2,1)}) %all-gather.11.cloned.1.call-update) | async-done | bytes 2097168 | tf_op jit(solution)/shard_map/all_gather | solution.py:128
  178.5 3.2 %gather_fusion.1 = bf16[64,4096]{1,0:T(8,128)(2,1)S(1)} fusion(bf16[256,4096]{1,0:T(8,128)(2,1)} %all-gather.11.cloned.1.call-done, s32[1024]{0:T(1024)S(1)} %pad_clamp_fusion), kind=kCustom, calls=%fused_computation.1.clone | custom fusion | bytes 1048832 | tf_op jit(solution)/shard_map/jit(_take)/gather | solution.py:95
  181.9 3.4 %collective-permute-start.1 = (bf16[64,4096]{1,0:T(8,128)(2,1)S(1)}, bf16[64,4096]{1,0:T(8,128)(2,1)S(1)}, u32[]{:S(2)}, u32[]{:S(2)}) collective-permute-start(bf16[64,4096]{1,0:T(8,128)(2,1)S(1)} %select_select_fusion), channel_id=1, source_target_pairs={{2,0},{4,2},{6,4},{8,6},{10,8},{12,10},{14,12},{3,1},{5,3},{7,5},{... | collective-permute-start | bytes 1572872 | tf_op jit(solution)/shard_map/ppermute | solution.py:17
  185.3 18.0 %all-gather.9.cloned.1.call-done = bf16[256,4096]{1,0:T(8,128)(2,1)} async-done(((bf16[64,4096]{1,0:T(8,128)(2,1)}), bf16[256,4096]{1,0:T(8,128)(2,1)}) %all-gather.9.cloned.1.call-update) | async-done | bytes 2097168 | tf_op jit(solution)/shard_map/all_gather | solution.py:127
  203.3 3.2 %gather_fusion = bf16[64,4096]{1,0:T(8,128)(2,1)S(1)} fusion(bf16[256,4096]{1,0:T(8,128)(2,1)} %all-gather.9.cloned.1.call-done, s32[1024]{0:T(1024)S(1)} %pad_clamp_fusion.1), kind=kCustom, calls=%fused_computation.clone | custom fusion | bytes 1048832 | tf_op jit(solution)/shard_map/jit(_take)/gather | solution.py:95
  206.6 3.4 %collective-permute-start = (bf16[64,4096]{1,0:T(8,128)(2,1)S(1)}, bf16[64,4096]{1,0:T(8,128)(2,1)S(1)}, u32[]{:S(2)}, u32[]{:S(2)}) collective-permute-start(bf16[64,4096]{1,0:T(8,128)(2,1)S(1)} %select_select_fusion.1), channel_id=1, source_target_pairs={{0,2},{2,4},{4,6},{6,8},{8,10},{10,12},{12,14},{1,3},{3,5},{5,7},{... | collective-permute-start | bytes 1572872 | tf_op jit(solution)/shard_map/ppermute | solution.py:17
  210.0 13.5 %collective-permute-done = bf16[64,4096]{1,0:T(8,128)(2,1)S(1)} collective-permute-done((bf16[64,4096]{1,0:T(8,128)(2,1)S(1)}, bf16[64,4096]{1,0:T(8,128)(2,1)S(1)}, u32[]{:S(2)}, u32[]{:S(2)}) %collective-permute-start) | collective-permute-done | bytes 524320 | tf_op jit(solution)/shard_map/ppermute | solution.py:17
  223.5 0.8 copy.53
  224.3 0.8 copy.54
  (97 shorter events, 8.3 us)
Async XLA Ops:
  7.2 26.2 %all-gather.17.cloned.1.call-start = ((), (), s32[]{:S(2)}) async-start(), calls=%async_computation.8 | async-start | bytes 2621440 | tf_op jit(solution)/shard_map/all_gather | solution.py:172
  7.9 49.6 %all-gather.15.cloned.1.call-start = ((), (), s32[]{:S(2)}) async-start(), calls=%async_computation.7 | async-start | bytes 2621440 | tf_op jit(solution)/shard_map/all_gather | solution.py:173
  8.6 79.6 %all-gather.13.cloned.1.call-start = ((), (), s32[]{:S(2)}) async-start(), calls=%async_computation.6 | async-start | bytes 2621440 | tf_op jit(solution)/shard_map/all_gather | solution.py:171
  9.4 113.6 %reduce-scatter.5.cloned.1.call-start = ((), (), s32[]{:S(2)}) async-start(), calls=%async_computation.4 | async-start | bytes 2621440 | tf_op jit(solution)/shard_map/reduce_scatter | solution.py:186
  88.0 65.9 %reduce-scatter.3.cloned.1.call-start = ((), (), s32[]{:S(2)}) async-start(), calls=%async_computation.2 | async-start | bytes 2621440 | tf_op jit(solution)/shard_map/reduce_scatter | solution.py:180
  90.3 32.7 %copy-start = (bf16[1,1,64,4096]{3,2,1,0:T(8,128)(2,1)S(1)}, bf16[1,1,64,4096]{3,2,1,0:T(8,128)(2,1)}, u32[]{:S(2)}) copy-start(bf16[1,1,64,4096]{3,2,1,0:T(8,128)(2,1)} %param.12) | copy-start | bytes 1572868
  121.1 3.3 %copy-start.2 = (bf16[1,1,64,4096]{3,2,1,0:T(8,128)(2,1)S(1)}, bf16[1,1,64,4096]{3,2,1,0:T(8,128)(2,1)}, u32[]{:S(2)}) copy-start(bf16[1,1,64,4096]{3,2,1,0:T(8,128)(2,1)} %param.13) | copy-start | bytes 1572868
  121.1 32.8 %copy-start.1 = (bf16[1,1,64,4096]{3,2,1,0:T(8,128)(2,1)S(1)}, bf16[1,1,64,4096]{3,2,1,0:T(8,128)(2,1)}, u32[]{:S(2)}) copy-start(bf16[1,1,64,4096]{3,2,1,0:T(8,128)(2,1)} %param.11) | copy-start | bytes 1572868
  121.1 57.4 %all-gather.11.cloned.1.call-start = ((), (), s32[]{:S(2)}) async-start(), calls=%async_computation.5 | async-start | bytes 2621440 | tf_op jit(solution)/shard_map/all_gather | solution.py:128
  126.7 76.6 %all-gather.9.cloned.1.call-start = ((), (), s32[]{:S(2)}) async-start(), calls=%async_computation.3 | async-start | bytes 2621440 | tf_op jit(solution)/shard_map/all_gather | solution.py:127
  181.9 28.1 %collective-permute-start.1 = (bf16[64,4096]{1,0:T(8,128)(2,1)S(1)}, bf16[64,4096]{1,0:T(8,128)(2,1)S(1)}, u32[]{:S(2)}, u32[]{:S(2)}) collective-permute-start(bf16[64,4096]{1,0:T(8,128)(2,1)S(1)} %select_select_fusion), channel_id=1, source_target_pairs={{2,0},{4,2},{6,4},{8,6},{10,8},{12,10},{14,12},{3,1},{5,3},{7,5},{... | collective-permute-start | bytes 1572872 | tf_op jit(solution)/shard_map/ppermute | solution.py:17
  206.6 16.9 %collective-permute-start = (bf16[64,4096]{1,0:T(8,128)(2,1)S(1)}, bf16[64,4096]{1,0:T(8,128)(2,1)S(1)}, u32[]{:S(2)}, u32[]{:S(2)}) collective-permute-start(bf16[64,4096]{1,0:T(8,128)(2,1)S(1)} %select_select_fusion.1), channel_id=1, source_target_pairs={{0,2},{2,4},{4,6},{6,8},{8,10},{10,12},{12,14},{1,3},{3,5},{5,7},{... | collective-permute-start | bytes 1572872 | tf_op jit(solution)/shard_map/ppermute | solution.py:17
Sparse Core Ops, SparseCore 0:
  9.6 23.7 all-gather.16
  34.9 22.5 all-gather.14
  59.1 22.5 all-gather.12
  88.1 31.6 reduce-scatter.4
  122.3 31.5 reduce-scatter.2
  155.9 22.5 all-gather.10
  180.6 22.5 all-gather.8
where the time goes:
time: 232 us
  waiting for transfers between devices  106 us (46%)
  matrix products  77.1 us (33%)
  other arithmetic  14.4 us (6%)
  between operations  14.4 us (6%)
  local copies, waits for them, and re-layouts  12.8 us (6%)
  starting transfers between devices  7.19 us (3%)
    dot_general x1, matrix products, local(): jnp.dot(hidden, w_down, preferred_element_type=jnp.float32)  30.8 us
    dot_general x1, matrix products, against_rows(): lax.dot_general(left, right, (((1,), (1,)), ((), ())), preferred_element_...  30.4 us
    reduce_scatter x1, waiting for transfers between devices, local(): lax.psum_scatter(jnp.dot(hidden, w_down, preferred_element_type=jnp.float...  25.9 us
    all_gather x1, waiting for transfers between devices, route_rows(): lax.all_gather(own_grad, ('rep', 'tp'), axis=0, tiled=True)  20.4 us
    all_gather x1, waiting for transfers between devices, local(): lax.all_gather(saved_own, ('rep', 'tp'), axis=0, tiled=True)  19.9 us
    all_gather x1, waiting for transfers between devices, route_rows(): lax.all_gather(own_result, ('rep', 'tp'), axis=0, tiled=True)  18 us
    dot_general x1, matrix products, local(): jnp.dot(normalize(saved, gain_row), w_up, preferred_element_type=jnp.floa...  15.9 us
    ppermute x2, waiting for transfers between devices, from_behind(): return lax.ppermute(block, axis, route)  13.5 us
  transfers between devices with their start and end apart: 9, of which 6 were waited for; matrix products, arithmetic and copies ran while one was open for 44% of the time, Pallas kernels for 0%

commit v1 on v0

v1 whole, which is shorter than its diff:
```python
import functools

import jax
import jax.numpy as jnp
from jax import lax
from jax.experimental import pallas as pl
from jax.experimental.pallas import tpu as pltpu
from jax.sharding import PartitionSpec as P

BLOCK = 16
CAPB = 8
START = 5
EPSILON = 1e-05
VMEM_LIMIT = 52 * 1024 * 1024


def from_behind(block, axis, distance):
    devices = range(lax.axis_size(axis))
    route = [(i - distance, i) for i in devices if i - distance in devices]
    return lax.ppermute(block, axis, route)


def plan_kernel(replicas, per_shard, where_ref, layers_ref, count_ref, dest_ref, out_ref):
    bounds = layers_ref.shape[0] - 1
    position = where_ref[0]
    zero = jnp.int32(0)
    ends, seen = [], jnp.int32(-1)
    for s in range(bounds):
        seen = seen + layers_ref[s]
        ends.append(seen)
    moved = [
        [
            jnp.where((dest_ref[s, r] != r) & (count_ref[s, r] > 0), count_ref[s, r], 0)
            for r in range(replicas)
        ]
        for s in range(bounds)
    ]

    def place(replica, block):
        return (lax.div(block, per_shard) * replicas + replica) * per_shard + lax.rem(block, per_shard)

    for which in range(2):
        at = position if which == 0 else jnp.maximum(position - 1, 0)
        live = [jnp.int32(START) for _ in range(replicas)]
        mine = [zero for _ in range(replicas)]
        to = [jnp.int32(r) for r in range(replicas)]
        for s in range(bounds):
            before, here = ends[s] < at, ends[s] == at
            for q in range(replicas):
                gain = -moved[s][q]
                for r in range(replicas):
                    gain = gain + jnp.where(dest_ref[s, r] == q, moved[s][r], 0)
                live[q] = live[q] + jnp.where(before, gain, 0)
                mine[q] = jnp.where(here, moved[s][q], mine[q])
                to[q] = jnp.where(here, dest_ref[s, q], to[q])
        incoming = [
            sum((jnp.where(to[r] == q, mine[r], 0) for r in range(replicas)), zero)
            for q in range(replicas)
        ]
        offset = [
            sum((jnp.where(to[o] == to[r], mine[o], 0) for o in range(r)), zero)
            for r in range(replicas)
        ]
        filled = zero
        for q in range(replicas):
            for k in range(CAPB):
                local = k - incoming[q]
                own = (local >= 0) & (local < live[q] - mine[q])
                source = jnp.where(own, place(jnp.int32(q), jnp.maximum(local + mine[q], 0)), -1)
                for r in range(replicas):
                    hit = (mine[r] > 0) & (to[r] == q) & (k >= offset[r]) & (k < offset[r] + mine[r])
                    source = jnp.where(
                        hit, place(jnp.int32(r), jnp.maximum(k - offset[r], 0)), source
                    )
                target = place(jnp.int32(q), jnp.int32(k))
                out_ref[2 * which, filled] = jnp.maximum(source, 0)
                out_ref[2 * which + 1, filled] = target
                filled = filled + jnp.where(source >= 0, 1, 0)


def make_plan(where, section_layers, redirect_count, redirect_dest, replicas, per_shard):
    return pl.pallas_call(
        functools.partial(plan_kernel, replicas, per_shard),
        out_shape=jax.ShapeDtypeStruct((4, replicas * CAPB + 1), jnp.int32),
        in_specs=[pl.BlockSpec(memory_space=pltpu.SMEM)] * 4,
        out_specs=pl.BlockSpec(memory_space=pltpu.SMEM),
    )(where, section_layers, redirect_count, redirect_dest)


def normalize(values, gain_row):
    wide = values.astype(jnp.float32)
    scale = lax.rsqrt(jnp.mean(wide * wide, axis=-1, keepdims=True) + EPSILON)
    return (wide * scale * gain_row.astype(jnp.float32)).astype(jnp.bfloat16)


def norm_back(values, gain_row, upstream):
    wide = values.astype(jnp.float32)
    scale = lax.rsqrt(jnp.mean(wide * wide, axis=-1, keepdims=True) + EPSILON)
    weighted = gain_row.astype(jnp.float32) * upstream
    return scale * weighted - wide * (scale * scale * scale) * jnp.mean(
        weighted * wide, axis=-1, keepdims=True
    )


def silu_slope(upper):
    sigma = jax.nn.sigmoid(upper)
    return sigma * (1.0 + upper * (1.0 - sigma))


def dot(left, right, contract):
    return lax.dot_general(
        left, right, ((contract[:1], contract[1:]), ((), ())), preferred_element_type=jnp.float32
    )


def rows_of(block):
    return pl.ds(pl.multiple_of(block * BLOCK, BLOCK), BLOCK)


def forward_kernel(
    blocks, per_shard, plan_ref, where_ref, fresh_ref, gain_ref, up_ref, down_ref,
    sum_ref, mine_ref, normed, total,
):
    step = pl.program_id(0)

    @pl.when(step == 0)
    def _():
        total[...] = jnp.zeros_like(total)
        mine_ref[...] = jnp.zeros_like(mine_ref)

        @pl.loop(0, blocks)
        def _(b):
            values = fresh_ref[rows_of(plan_ref[0, b]), :]
            normed[rows_of(b), :] = normalize(values, gain_ref[...])
            local = plan_ref[1, b] - where_ref[1] * per_shard

            @pl.when((local >= 0) & (local < per_shard))
            def _():
                mine_ref[rows_of(local), :] = values

    hidden = jax.nn.silu(dot(normed[...], up_ref[...], (1, 0))).astype(jnp.bfloat16)
    total[...] += dot(hidden, down_ref[...], (1, 0))

    @pl.when(step == pl.num_programs(0) - 1)
    def _():
        sum_ref[...] = jnp.zeros_like(sum_ref)

        @pl.loop(0, blocks)
        def _(b):
            sum_ref[rows_of(plan_ref[1, b]), :] = total[rows_of(b), :].astype(jnp.bfloat16)


def backward_kernel(
    blocks, per_shard, plan_ref, where_ref, saved_ref, grad_ref, gain_ref, up_ref, down_ref,
    sum_ref, mine_saved_ref, mine_grad_ref, normed, upstream, total,
):
    step = pl.program_id(0)

    @pl.when(step == 0)
    def _():
        total[...] = jnp.zeros_like(total)
        mine_saved_ref[...] = jnp.zeros_like(mine_saved_ref)
        mine_grad_ref[...] = jnp.zeros_like(mine_grad_ref)

        @pl.loop(0, blocks)
        def _(b):
            source = rows_of(plan_ref[3, b])
            values = saved_ref[source, :]
            grads = grad_ref[source, :]
            normed[rows_of(b), :] = normalize(values, gain_ref[...])
            upstream[rows_of(b), :] = grads
            local = plan_ref[2, b] - where_ref[1] * per_shard

            @pl.when((local >= 0) & (local < per_shard))
            def _():
                mine_saved_ref[rows_of(local), :] = values
                mine_grad_ref[rows_of(local), :] = grads

    upper = dot(normed[...], up_ref[...], (1, 0))
    back = (dot(upstream[...], down_ref[...], (1, 1)) * silu_slope(upper)).astype(jnp.bfloat16)
    total[...] += dot(back, up_ref[...], (1, 1))

    @pl.when(step == pl.num_programs(0) - 1)
    def _():
        sum_ref[...] = jnp.zeros_like(sum_ref)

        @pl.loop(0, blocks)
        def _(b):
            sum_ref[rows_of(plan_ref[2, b]), :] = total[rows_of(b), :].astype(jnp.bfloat16)


def run_layer(kernel, plan, where, arrays, gain, w_up, w_down, blocks, shard_rows, products):
    every, width = arrays[0].shape
    hidden = w_up.shape[1]
    tile = next(t for t in (512, 256, 128, hidden) if hidden % t == 0)
    rows = blocks * BLOCK
    whole = lambda shape: pl.BlockSpec(shape, lambda i, *_: (0, 0))
    n = len(arrays)
    return pl.pallas_call(
        functools.partial(kernel, blocks, shard_rows // BLOCK),
        grid_spec=pltpu.PrefetchScalarGridSpec(
            num_scalar_prefetch=2,
            grid=(hidden // tile,),
            in_specs=[whole((every, width))] * n
            + [
                whole((1, width)),
                pl.BlockSpec((width, tile), lambda i, *_: (0, i)),
                pl.BlockSpec((tile, width), lambda i, *_: (i, 0)),
            ],
            out_specs=[whole((every, width))] + [whole((shard_rows, width))] * n,
            scratch_shapes=[pltpu.VMEM((rows, width), jnp.bfloat16)] * n
            + [pltpu.VMEM((rows, width), jnp.float32)],
        ),
        out_shape=[jax.ShapeDtypeStruct((every, width), jnp.bfloat16)]
        + [jax.ShapeDtypeStruct((shard_rows, width), jnp.bfloat16)] * n,
        compiler_params=pltpu.CompilerParams(
            dimension_semantics=("arbitrary",), vmem_limit_bytes=VMEM_LIMIT
        ),
        cost_estimate=pl.CostEstimate(
            flops=2 * products * rows * width * hidden,
            bytes_accessed=4 * width * hidden,
            transcendentals=rows * hidden,
        ),
    )(plan, where, *arrays, gain, w_up, w_down)


def gather(own):
    return lax.all_gather(
        lax.all_gather(own, "rep", axis=0, tiled=True), "tp", axis=0, tiled=True
    )


def scatter(partial):
    near = lax.psum_scatter(partial, "tp", scatter_dimension=0, tiled=True)
    return lax.psum_scatter(near, "rep", scatter_dimension=0, tiled=True).astype(jnp.float32)


def local(
    act_forward,
    act_saved,
    grad_output,
    norm_gain,
    up_weight,
    down_weight,
    section_layers,
    redirect_count,
    redirect_dest,
):
    replicas = lax.axis_size("rep")
    shard_rows, width = act_forward.shape[2:]
    per_shard = shard_rows // BLOCK
    blocks = START * replicas
    shard = lax.axis_index("tp") * replicas + lax.axis_index("rep")
    where = jnp.stack([lax.axis_index("pipe"), shard]).astype(jnp.int32)
    plan = make_plan(where, section_layers, redirect_count, redirect_dest, replicas, per_shard)
    w_up, w_down = up_weight[0], down_weight[0]
    fresh = gather(act_forward[0, 0])
    saved = gather(act_saved[0, 0])
    upstream = gather(grad_output[0, 0])
    mixed, mine_fresh = run_layer(
        forward_kernel, plan, where, [fresh], norm_gain, w_up, w_down, blocks, shard_rows, 2
    )
    returned, mine_saved, mine_grad = run_layer(
        backward_kernel, plan, where, [saved, upstream], norm_gain, w_up, w_down, blocks, shard_rows, 3
    )
    result = (mine_fresh.astype(jnp.float32) + scatter(mixed)).astype(jnp.bfloat16)
    arrive_forward = from_behind(result, "pipe", 1)
    gradient = (
        mine_grad.astype(jnp.float32) + norm_back(mine_saved, norm_gain, scatter(returned))
    ).astype(jnp.bfloat16)
    arrive_backward = from_behind(gradient, "pipe", -1)
    return (arrive_forward[None, None], arrive_backward[None, None])


def solution(mesh):
    in_specs = (
        P("pipe", "rep", "tp", None),
        P("pipe", "rep", "tp", None),
        P("pipe", "rep", "tp", None),
        P("pipe", None),
        P("pipe", None, ("rep", "tp")),
        P("pipe", ("rep", "tp"), None),
        P(),
        P(),
        P(),
    )
    out_specs = (P("pipe", "rep", "tp", None), P("pipe", "rep", "tp", None))
    return jax.shard_map(local, mesh=mesh, in_specs=in_specs, out_specs=out_specs, check_vma=False)
```

time: 232 us -> 249 us (1.073)
  matrix products: 77.1 us -> 0 us
  Pallas kernels: 0 us -> 61.8 us
  waiting for transfers between devices: 106 us -> 156 us
  other arithmetic: 14.4 us -> 4.65 us
  local copies, waits for them, and re-layouts: 12.8 us -> 4.87 us
    dot_general x3 -> x0, matrix products: 77.1 us -> none  [the longest x1 30.8 us: local(): jnp.dot(hidden, w_down, preferred_element_type=jnp.float32)]
    pallas_call x0 -> x3, Pallas kernels: none -> 61.8 us  [the longest x2 60 us: run_layer(): pl.pallas_call(functools.partial(kernel, blocks, shard_rows // BLOCK), gr...]
    all_gather x5 -> x6, waiting for transfers between devices: 64.5 us -> 89.8 us  [the longest x3 68.2 us: gather(): lax.all_gather(own, 'rep', axis=0, tiled=True)]
    reduce_scatter x2 -> x4, waiting for transfers between devices: 25.9 us -> 50 us  [the longest x2 39.8 us: scatter(): lax.psum_scatter(near, 'rep', scatter_dimension=0, tiled=True)]
    gather x2 -> x0, local copies, waits for them, and re-layouts: 6.46 us -> none  [pick_rows(): taken = jnp.take(values, jnp.maximum(index, 0), axis=0)]
    reduce_sum x14 -> x0, other arithmetic: 5.42 us -> none  [the longest x2 4.17 us: normalize(): scale = lax.rsqrt(jnp.mean(wide * wide, axis=-1, keepdims=True) + EPSILON)]
  transfers between devices with their start and end apart: 9 -> 12, of which waited for: 6 -> 9; matrix products, arithmetic and copies ran while one was open for 44% -> 2% of each run, Pallas kernels for 0% -> 25%
where the time goes in v1:
time: 249 us; the launch traced here: 248 us
  waiting for transfers between devices  156 us (63%)
  Pallas kernels  61.8 us (25%)
  between operations  14.3 us (6%)
  starting transfers between devices  7.13 us (3%)
  local copies, waits for them, and re-layouts  4.87 us (2%)
  other arithmetic  4.65 us (2%)
    all_gather x3, waiting for transfers between devices, gather(): lax.all_gather(own, 'rep', axis=0, tiled=True)  68.2 us
    pallas_call x2, Pallas kernels, run_layer(): pl.pallas_call(functools.partial(kernel, blocks, shard_rows // BLOCK), gr...  60 us
    reduce_scatter x2, waiting for transfers between devices, scatter(): lax.psum_scatter(near, 'rep', scatter_dimension=0, tiled=True)  39.8 us
    all_gather x3, waiting for transfers between devices, gather(): lax.all_gather(lax.all_gather(own, 'rep', axis=0, tiled=True), 'tp', axis...  21.6 us
    ppermute x2, waiting for transfers between devices, from_behind(): return lax.ppermute(block, axis, route)  13.1 us
    reduce_scatter x2, waiting for transfers between devices, scatter(): near = lax.psum_scatter(partial, 'tp', scatter_dimension=0, tiled=True)  10.2 us
    ppermute x2, starting transfers between devices, from_behind(): return lax.ppermute(block, axis, route)  6.74 us
  transfers between devices with their start and end apart: 12, of which 9 were waited for; matrix products, arithmetic and copies ran while one was open for 2% of the time, Pallas kernels for 25%

profile of v1, /device:TPU:8, one launch (start us, length us, event | category | flops | bytes accessed | tf_op | source)
XLA Modules:
  0.0 248.4 jit_solution(16258105069725105693)
XLA Ops:
  7.2 0.7 all-gather.17.cloned.1.call-update
  8.0 0.7 all-gather.21.cloned.1.call-update
  8.7 0.7 all-gather.13.cloned.1.call-update
  9.5 22.6 %all-gather.17.cloned.1.call-done = bf16[1,1,128,4096]{3,2,1,0:T(8,128)(2,1)} async-done(((bf16[1,1,64,4096]{3,2,1,0:T(8,128)(2,1)}), bf16[1,1,128,4096]{3,2,1,0:T(8,128)(2,1)}) %all-gather.17.cloned.1.call-update) | async-done | bytes 1048592 | tf_op jit(solution)/shard_map/all_gather | solution.py:229
  32.1 22.8 %all-gather.21.cloned.1.call-done = bf16[1,1,128,4096]{3,2,1,0:T(8,128)(2,1)} async-done(((bf16[1,1,64,4096]{3,2,1,0:T(8,128)(2,1)}), bf16[1,1,128,4096]{3,2,1,0:T(8,128)(2,1)}) %all-gather.21.cloned.1.call-update) | async-done | bytes 1048592 | tf_op jit(solution)/shard_map/all_gather | solution.py:229
  55.0 22.8 %all-gather.13.cloned.1.call-done = bf16[1,1,128,4096]{3,2,1,0:T(8,128)(2,1)} async-done(((bf16[1,1,64,4096]{3,2,1,0:T(8,128)(2,1)}), bf16[1,1,128,4096]{3,2,1,0:T(8,128)(2,1)}) %all-gather.13.cloned.1.call-update) | async-done | bytes 1048592 | tf_op jit(solution)/shard_map/all_gather | solution.py:229
  79.9 1.8 shard_map.104.plan_ref
  81.7 8.4 %all-gather.19.cloned.1.call-done = bf16[1,1,256,4096]{3,2,1,0:T(8,128)(2,1)} async-done(((bf16[1,1,128,4096]{3,2,1,0:T(8,128)(2,1)}), bf16[1,1,256,4096]{3,2,1,0:T(8,128)(2,1)}) %all-gather.19.cloned.1.call-update) | async-done | bytes 2097168 | tf_op jit(solution)/shard_map/all_gather | solution.py:228
  90.1 13.2 %all-gather.23.cloned.1.call-done = bf16[1,1,256,4096]{3,2,1,0:T(8,128)(2,1)} async-done(((bf16[1,1,128,4096]{3,2,1,0:T(8,128)(2,1)}), bf16[1,1,256,4096]{3,2,1,0:T(8,128)(2,1)}) %all-gather.23.cloned.1.call-update) | async-done | bytes 2097168 | tf_op jit(solution)/shard_map/all_gather | solution.py:228
  103.3 0.7 copy-done.1
  104.0 0.7 copy-done.3
  104.6 34.3 %shard_map.106 = (bf16[256,4096]{1,0:T(8,128)(2,1)}, bf16[64,4096]{1,0:T(8,128)(2,1)S(1)}, bf16[64,4096]{1,0:T(8,128)(2,1)S(1)}) custom-call(s32[4,17]{1,0:T(4,128)S(1)} %copy-done.1, s32[2]{0:T(128)S(1)} %copy-done.3, bf16[256,4096]{1,0:T(8,128)(2,1)} %bitcast.14, bf16[256,4096]{1,0:T(8,128)(2,1)} %bitcast.16, bf16[1,4096]{1,0:T(2,128)(2,1)S(1)} %copy-done, ...), custom_call_target="tpu_custom_call" | custom-call | flops 14092861440 | bytes 58720256 | tf_op jit(solution)/shard_map/pallas_call | solution.py:199
  139.7 25.7 %shard_map.105 = (bf16[256,4096]{1,0:T(8,128)(2,1)}, bf16[64,4096]{1,0:T(8,128)(2,1)S(1)}) custom-call(s32[4,17]{1,0:T(4,128)S(1)} %copy-done.2, s32[2]{0:T(128)S(1)} %copy-done.4, bf16[256,4096]{1,0:T(8,128)(2,1)} %bitcast.15, bf16[1,4096]{1,0:T(2,128)(2,1)S(1)} %copy-done, bf16[4096,3584]{1,0:T(8,128)(2,1)} %bitcast.11, bf16[3584,4096]{1,0:T(8,128)(2,1)} %bitcast.13), custom_call_target="tpu_custom_call" | custom-call | flops 9395240960 | bytes 58720256 | tf_op jit(solution)/shard_map/pallas_call | solution.py:199
  166.2 10.2 %reduce-scatter.5.cloned.1.call-done = bf16[128,4096]{1,0:T(8,128)(2,1)} async-done(((bf16[256,4096]{1,0:T(8,128)(2,1)}), bf16[128,4096]{1,0:T(8,128)(2,1)}) %reduce-scatter.5.cloned.1.call-update) | async-done | bytes 1048592 | tf_op jit(solution)/shard_map/reduce_scatter | solution.py:234
  176.4 23.5 %reduce-scatter.11.cloned.1.call-done = bf16[64,4096]{1,0:T(8,128)(2,1)} async-done(((bf16[128,4096]{1,0:T(8,128)(2,1)}), bf16[64,4096]{1,0:T(8,128)(2,1)}) %reduce-scatter.11.cloned.1.call-update) | async-done | bytes 524304 | tf_op jit(solution)/shard_map/reduce_scatter | solution.py:235
  199.9 1.4 fusion
  201.3 1.4 fusion.4
  202.7 3.4 %collective-permute-start.1 = (bf16[64,4096]{1,0:T(8,128)(2,1)S(1)}, bf16[64,4096]{1,0:T(8,128)(2,1)S(1)}, u32[]{:S(2)}, u32[]{:S(2)}) collective-permute-start(bf16[64,4096]{1,0:T(8,128)(2,1)S(1)} %fusion.4), channel_id=1, source_target_pairs={{2,0},{4,2},{6,4},{8,6},{10,8},{12,10},{14,12},{3,1},{5,3},{7,5},{... | collective-permute-start | bytes 1572872 | tf_op jit(solution)/shard_map/ppermute | solution.py:20
  206.1 16.3 %reduce-scatter.7.cloned.1.call-done = bf16[64,4096]{1,0:T(8,128)(2,1)} async-done(((bf16[128,4096]{1,0:T(8,128)(2,1)}), bf16[64,4096]{1,0:T(8,128)(2,1)}) %reduce-scatter.7.cloned.1.call-update) | async-done | bytes 524304 | tf_op jit(solution)/shard_map/reduce_scatter | solution.py:235
  222.4 1.2 add_convert_fusion
  223.5 3.4 %collective-permute-start = (bf16[64,4096]{1,0:T(8,128)(2,1)S(1)}, bf16[64,4096]{1,0:T(8,128)(2,1)S(1)}, u32[]{:S(2)}, u32[]{:S(2)}) collective-permute-start(bf16[64,4096]{1,0:T(8,128)(2,1)S(1)} %add_convert_fusion), channel_id=1, source_target_pairs={{0,2},{2,4},{4,6},{6,8},{8,10},{10,12},{12,14},{1,3},{3,5},{5,7},{... | collective-permute-start | bytes 1572872 | tf_op jit(solution)/shard_map/ppermute | solution.py:20
  226.9 13.1 %collective-permute-done = bf16[64,4096]{1,0:T(8,128)(2,1)S(1)} collective-permute-done((bf16[64,4096]{1,0:T(8,128)(2,1)S(1)}, bf16[64,4096]{1,0:T(8,128)(2,1)S(1)}, u32[]{:S(2)}, u32[]{:S(2)}) %collective-permute-start) | collective-permute-done | bytes 524320 | tf_op jit(solution)/shard_map/ppermute | solution.py:20
  240.0 0.8 copy.15
  240.8 0.8 copy.16
  (37 shorter events, 3.8 us)
Async XLA Ops:
  7.2 24.9 %all-gather.17.cloned.1.call-start = ((), (), s32[]{:S(2)}) async-start(), calls=%async_computation.10 | async-start | bytes 1572864 | tf_op jit(solution)/shard_map/all_gather | solution.py:229
  7.9 70.0 %copy-start.5 = (s32[3,2]{0,1:T(2,128)S(1)}, s32[3,2]{0,1:T(2,128)}, u32[]{:S(2)}) copy-start(s32[3,2]{0,1:T(2,128)} %param.16) | copy-start | bytes 76
  7.9 70.7 %copy-start.6 = (s32[3,2]{0,1:T(2,128)S(1)}, s32[3,2]{0,1:T(2,128)}, u32[]{:S(2)}) copy-start(s32[3,2]{0,1:T(2,128)} %param.17) | copy-start | bytes 76
  7.9 95.3 %copy-start = (bf16[1,4096]{1,0:T(2,128)(2,1)S(1)}, bf16[1,4096]{1,0:T(2,128)(2,1)}, u32[]{:S(2)}) copy-start(bf16[1,4096]{1,0:T(2,128)(2,1)} %gain_ref.3) | copy-start | bytes 24580
  7.9 47.0 %all-gather.21.cloned.1.call-start = ((), (), s32[]{:S(2)}) async-start(), calls=%async_computation.12 | async-start | bytes 1572864 | tf_op jit(solution)/shard_map/all_gather | solution.py:229
  8.7 69.1 %all-gather.13.cloned.1.call-start = ((), (), s32[]{:S(2)}) async-start(), calls=%async_computation.8 | async-start | bytes 1572864 | tf_op jit(solution)/shard_map/all_gather | solution.py:229
  9.4 80.7 %all-gather.19.cloned.1.call-start = ((), (), s32[]{:S(2)}) async-start(), calls=%async_computation.11 | async-start | bytes 3145728 | tf_op jit(solution)/shard_map/all_gather | solution.py:228
  32.1 71.2 %all-gather.23.cloned.1.call-start = ((), (), s32[]{:S(2)}) async-start(), calls=%async_computation.13 | async-start | bytes 3145728 | tf_op jit(solution)/shard_map/all_gather | solution.py:228
  55.0 84.1 %all-gather.15.cloned.1.call-start = ((), (), s32[]{:S(2)}) async-start(), calls=%async_computation.9 | async-start | bytes 3145728 | tf_op jit(solution)/shard_map/all_gather | solution.py:228
  77.8 87.6 %reduce-scatter.9.cloned.1.call-start = ((), (), s32[]{:S(2)}) async-start(), calls=%async_computation.6 | async-start | bytes 3145728 | tf_op jit(solution)/shard_map/reduce_scatter | solution.py:234
  103.3 0.7 copy-start.1
  104.0 0.7 copy-start.3
  139.0 0.7 copy-start.2
  139.0 0.7 copy-start.4
  139.0 37.4 %reduce-scatter.5.cloned.1.call-start = ((), (), s32[]{:S(2)}) async-start(), calls=%async_computation.4 | async-start | bytes 3145728 | tf_op jit(solution)/shard_map/reduce_scatter | solution.py:234
  165.4 34.5 %reduce-scatter.11.cloned.1.call-start = ((), (), s32[]{:S(2)}) async-start(), calls=%async_computation.7 | async-start | bytes 1572864 | tf_op jit(solution)/shard_map/reduce_scatter | solution.py:235
  166.1 56.3 %reduce-scatter.7.cloned.1.call-start = ((), (), s32[]{:S(2)}) async-start(), calls=%async_computation.5 | async-start | bytes 1572864 | tf_op jit(solution)/shard_map/reduce_scatter | solution.py:235
  202.7 24.2 %collective-permute-start.1 = (bf16[64,4096]{1,0:T(8,128)(2,1)S(1)}, bf16[64,4096]{1,0:T(8,128)(2,1)S(1)}, u32[]{:S(2)}, u32[]{:S(2)}) collective-permute-start(bf16[64,4096]{1,0:T(8,128)(2,1)S(1)} %fusion.4), channel_id=1, source_target_pairs={{2,0},{4,2},{6,4},{8,6},{10,8},{12,10},{14,12},{3,1},{5,3},{7,5},{... | collective-permute-start | bytes 1572872 | tf_op jit(solution)/shard_map/ppermute | solution.py:20
  223.5 16.5 %collective-permute-start = (bf16[64,4096]{1,0:T(8,128)(2,1)S(1)}, bf16[64,4096]{1,0:T(8,128)(2,1)S(1)}, u32[]{:S(2)}, u32[]{:S(2)}) collective-permute-start(bf16[64,4096]{1,0:T(8,128)(2,1)S(1)} %add_convert_fusion), channel_id=1, source_target_pairs={{0,2},{2,4},{4,6},{6,8},{8,10},{10,12},{12,14},{1,3},{3,5},{5,7},{... | collective-permute-start | bytes 1572872 | tf_op jit(solution)/shard_map/ppermute | solution.py:20
Sparse Core Ops, SparseCore 0:
  9.5 22.4 all-gather.16
  33.6 21.2 all-gather.20
  56.5 21.2 all-gather.12
  79.2 10.8 all-gather.18
  91.5 11.7 all-gather.22
  104.7 11.7 all-gather.14
  139.1 10.8 reduce-scatter.8
  165.5 10.8 reduce-scatter.4
  178.6 21.2 reduce-scatter.10
  202.1 20.2 reduce-scatter.6

commit v2 on v1

--- a/solution.py
+++ b/solution.py
@@ -113,14 +113,28 @@
     )
 
 
+def for_source(block, per_shard, shard, arrays, body):
+    if len(arrays[0]) == 1:
+        body(*(pieces[0][rows_of(block), :] for pieces in arrays))
+        return
+    piece = lax.bitwise_xor(lax.div(block, per_shard), shard)
+    inside = rows_of(lax.rem(block, per_shard))
+    for i in range(len(arrays[0])):
+
+        @pl.when(piece == i)
+        def _():
+            body(*(pieces[i][inside, :] for pieces in arrays))
+
+
 def rows_of(block):
     return pl.ds(pl.multiple_of(block * BLOCK, BLOCK), BLOCK)
 
 
 def forward_kernel(
-    blocks, per_shard, plan_ref, where_ref, fresh_ref, gain_ref, up_ref, down_ref,
-    sum_ref, mine_ref, normed, total,
+    blocks, per_shard, parts, plan_ref, where_ref, *refs
 ):
+    fresh, refs = refs[:parts], refs[parts:]
+    gain_ref, up_ref, down_ref, sum_ref, mine_ref, normed, total = refs
     step = pl.program_id(0)
 
     @pl.when(step == 0)
@@ -130,13 +144,16 @@
 
         @pl.loop(0, blocks)
         def _(b):
-            values = fresh_ref[rows_of(plan_ref[0, b]), :]
-            normed[rows_of(b), :] = normalize(values, gain_ref[...])
             local = plan_ref[1, b] - where_ref[1] * per_shard
 
-            @pl.when((local >= 0) & (local < per_shard))
-            def _():
-                mine_ref[rows_of(local), :] = values
+            def place(values):
+                normed[rows_of(b), :] = normalize(values, gain_ref[...])
+
+                @pl.when((local >= 0) & (local < per_shard))
+                def _():
+                    mine_ref[rows_of(local), :] = values
+
+            for_source(plan_ref[0, b], per_shard, where_ref[1], [fresh], place)
 
     hidden = jax.nn.silu(dot(normed[...], up_ref[...], (1, 0))).astype(jnp.bfloat16)
     total[...] += dot(hidden, down_ref[...], (1, 0))
@@ -151,9 +168,11 @@
 
 
 def backward_kernel(
-    blocks, per_shard, plan_ref, where_ref, saved_ref, grad_ref, gain_ref, up_ref, down_ref,
-    sum_ref, mine_saved_ref, mine_grad_ref, normed, upstream, total,
+    blocks, per_shard, parts, plan_ref, where_ref, *refs
 ):
+    saved, grad, refs = refs[:parts], refs[parts : 2 * parts], refs[2 * parts :]
+    gain_ref, up_ref, down_ref, sum_ref, mine_saved_ref, mine_grad_ref = refs[:6]
+    normed, upstream, total = refs[6:]
     step = pl.program_id(0)
 
     @pl.when(step == 0)
@@ -164,17 +183,18 @@
 
         @pl.loop(0, blocks)
         def _(b):
-            source = rows_of(plan_ref[3, b])
-            values = saved_ref[source, :]
-            grads = grad_ref[source, :]
-            normed[rows_of(b), :] = normalize(values, gain_ref[...])
-            upstream[rows_of(b), :] = grads
             local = plan_ref[2, b] - where_ref[1] * per_shard
 
-            @pl.when((local >= 0) & (local < per_shard))
-            def _():
-                mine_saved_ref[rows_of(local), :] = values
-                mine_grad_ref[rows_of(local), :] = grads
+            def place(values, grads):
+                normed[rows_of(b), :] = normalize(values, gain_ref[...])
+                upstream[rows_of(b), :] = grads
+
+                @pl.when((local >= 0) & (local < per_shard))
+                def _():
+                    mine_saved_ref[rows_of(local), :] = values
+                    mine_grad_ref[rows_of(local), :] = grads
+
+            for_source(plan_ref[3, b], per_shard, where_ref[1], [saved, grad], place)
 
     upper = dot(normed[...], up_ref[...], (1, 0))
     back = (dot(upstream[...], down_ref[...], (1, 1)) * silu_slope(upper)).astype(jnp.bfloat16)
@@ -190,18 +210,20 @@
 
 
 def run_layer(kernel, plan, where, arrays, gain, w_up, w_down, blocks, shard_rows, products):
-    every, width = arrays[0].shape
+    parts = len(arrays[0])
+    piece_rows, width = arrays[0][0].shape
+    every = parts * piece_rows
     hidden = w_up.shape[1]
     tile = next(t for t in (512, 256, 128, hidden) if hidden % t == 0)
     rows = blocks * BLOCK
     whole = lambda shape: pl.BlockSpec(shape, lambda i, *_: (0, 0))
     n = len(arrays)
     return pl.pallas_call(
-        functools.partial(kernel, blocks, shard_rows // BLOCK),
+        functools.partial(kernel, blocks, shard_rows // BLOCK, parts),
         grid_spec=pltpu.PrefetchScalarGridSpec(
             num_scalar_prefetch=2,
             grid=(hidden // tile,),
-            in_specs=[whole((every, width))] * n
+            in_specs=[whole((piece_rows, width))] * (n * parts)
             + [
                 whole((1, width)),
                 pl.BlockSpec((width, tile), lambda i, *_: (0, i)),
@@ -221,18 +243,54 @@
             bytes_accessed=4 * width * hidden,
             transcendentals=rows * hidden,
         ),
-    )(plan, where, *arrays, gain, w_up, w_down)
-
-
-def gather(own):
-    return lax.all_gather(
-        lax.all_gather(own, "rep", axis=0, tiled=True), "tp", axis=0, tiled=True
-    )
+    )(plan, where, *(piece for pieces in arrays for piece in pieces), gain, w_up, w_down)
+
+
+def other(block, axis):
+    return lax.ppermute(block, axis, [(0, 1), (1, 0)])
+
+
+def in_pairs():
+    return lax.axis_size("rep") == 2 and lax.axis_size("tp") == 2
+
+
+def gather(own, across=None):
+    if in_pairs():
+        across = other(own, "rep") if across is None else across
+        return [own, across, other(own, "tp"), other(across, "tp")]
+    return [
+        lax.all_gather(lax.all_gather(own, "rep", axis=0, tiled=True), "tp", axis=0, tiled=True)
+    ]
+
+
+def half(block, index):
+    rows = block.shape[0] // 2
+    return lax.dynamic_slice_in_dim(block, index * rows, rows)
 
 
 def scatter(partial):
+    if in_pairs():
+        for axis in ("tp", "rep"):
+            index = lax.axis_index(axis)
+            arrived = other(half(partial, 1 - index), axis)
+            partial = half(partial, index).astype(jnp.float32) + arrived.astype(jnp.float32)
+            if axis == "tp":
+                partial = partial.astype(jnp.bfloat16)
+        return partial
     near = lax.psum_scatter(partial, "tp", scatter_dimension=0, tiled=True)
     return lax.psum_scatter(near, "rep", scatter_dimension=0, tiled=True).astype(jnp.float32)
+
+
+def scatter_direct(partial, shard, shard_rows):
+    if not in_pairs():
+        return scatter(partial), []
+    piece = lambda k: lax.dynamic_slice_in_dim(partial, lax.bitwise_xor(shard, k) * shard_rows, shard_rows)
+    arrived = [
+        other(piece(1), "rep"),
+        lax.ppermute(piece(3), ("rep", "tp"), [(i, 3 - i) for i in range(4)]),
+        other(piece(2), "tp"),
+    ]
+    return piece(0).astype(jnp.float32), arrived
 
 
 def local(
@@ -254,16 +312,25 @@
     where = jnp.stack([lax.axis_index("pipe"), shard]).astype(jnp.int32)
     plan = make_plan(where, section_layers, redirect_count, redirect_dest, replicas, per_shard)
     w_up, w_down = up_weight[0], down_weight[0]
-    fresh = gather(act_forward[0, 0])
-    saved = gather(act_saved[0, 0])
-    upstream = gather(grad_output[0, 0])
+    fresh_own, saved_own, grad_own = act_forward[0, 0], act_saved[0, 0], grad_output[0, 0]
+    fresh_across = None
+    if in_pairs():
+        fresh_across, saved_own, grad_own = lax.optimization_barrier(
+            (other(fresh_own, "rep"), saved_own, grad_own)
+        )
+    fresh = gather(fresh_own, fresh_across)
+    saved, upstream = gather(saved_own), gather(grad_own)
     mixed, mine_fresh = run_layer(
         forward_kernel, plan, where, [fresh], norm_gain, w_up, w_down, blocks, shard_rows, 2
     )
+    mixed, plan = lax.optimization_barrier((mixed, plan))
+    total, arrived = scatter_direct(mixed, shard, shard_rows)
     returned, mine_saved, mine_grad = run_layer(
         backward_kernel, plan, where, [saved, upstream], norm_gain, w_up, w_down, blocks, shard_rows, 3
     )
-    result = (mine_fresh.astype(jnp.float32) + scatter(mixed)).astype(jnp.bfloat16)
+    for block in arrived:
+        total = total + block.astype(jnp.float32)
+    result = (mine_fresh.astype(jnp.float32) + total).astype(jnp.bfloat16)
     arrive_forward = from_behind(result, "pipe", 1)
     gradient = (
         mine_grad.astype(jnp.float32) + norm_back(mine_saved, norm_gain, scatter(returned))

time: 249 us -> 165 us (0.66)
  waiting for transfers between devices: 156 us -> 69.1 us
  between operations: 14.3 us -> 0.82 us
  local copies, waits for them, and re-layouts: 4.87 us -> 13 us
  starting transfers between devices: 7.13 us -> 15.2 us
    all_gather x6 -> x0, waiting for transfers between devices: 89.8 us -> none  [the longest x3 68.2 us: gather(): lax.all_gather(own, 'rep', axis=0, tiled=True)]
    ppermute x0 -> x14, waiting for transfers between devices: none -> 55.6 us  [the longest x13 47 us: other(): return lax.ppermute(block, axis, [(0, 1), (1, 0)])]
    reduce_scatter x4 -> x0, waiting for transfers between devices: 50 us -> none  [the longest x2 39.8 us: scatter(): lax.psum_scatter(near, 'rep', scatter_dimension=0, tiled=True)]
    ppermute x0 -> x14, starting transfers between devices: none -> 8.54 us  [the longest x13 7.02 us: other(): return lax.ppermute(block, axis, [(0, 1), (1, 0)])]
    unnamed x18 -> x34, local copies, waits for them, and re-layouts: 4.87 us -> 10.1 us
    dynamic_slice x0 -> x3, local copies, waits for them, and re-layouts: none -> 2.97 us  [the longest x1 1.61 us: scatter_direct(): lax.dynamic_slice_in_dim(partial, lax.bitwise_xor(shard, k) * shard_rows,...]
    unnamed x10 -> x0, waiting for transfers between devices: 2.81 us -> none
  transfers between devices with their start and end apart: 12 -> 16, of which waited for: 9 -> 8; matrix products, arithmetic and copies ran while one was open for 2% -> 5% of each run, Pallas kernels for 25% -> 17%
where the time goes in v2:
time: 165 us; the launch traced here: 164 us
  waiting for transfers between devices  69.1 us (42%)
  Pallas kernels  61.4 us (37%)
  starting transfers between devices  15.2 us (9%)
  local copies, waits for them, and re-layouts  13 us (8%)
  other arithmetic  4.36 us (3%)
    pallas_call x2, Pallas kernels, run_layer(): pl.pallas_call(functools.partial(kernel, blocks, shard_rows // BLOCK, par...  59.7 us
    ppermute x13, waiting for transfers between devices, other(): return lax.ppermute(block, axis, [(0, 1), (1, 0)])  47 us
    ppermute x2, waiting for transfers between devices, from_behind(): return lax.ppermute(block, axis, route)  13.5 us
    unnamed x34, local copies, waits for them, and re-layouts  10.1 us
    ppermute x1, waiting for transfers between devices, scatter_direct(): lax.ppermute(piece(3), ('rep', 'tp'), [(i, 3 - i) for i in range(4)])  8.62 us
    ppermute x13, starting transfers between devices, other(): return lax.ppermute(block, axis, [(0, 1), (1, 0)])  7.02 us
    ppermute x2, starting transfers between devices, from_behind(): return lax.ppermute(block, axis, route)  6.68 us
  transfers between devices with their start and end apart: 16, of which 8 were waited for; matrix products, arithmetic and copies ran while one was open for 5% of the time, Pallas kernels for 17%

profile of v2, /device:TPU:8, one launch (start us, length us, event | category | flops | bytes accessed | tf_op | source)
XLA Modules:
  0.0 163.9 jit_solution(1617850247701063439)
XLA Ops:
  0.6 1.6 collective-permute-start
  2.2 12.4 %collective-permute-done.refs_1_ = bf16[64,4096]{1,0:T(8,128)(2,1)S(1)} collective-permute-done((bf16[64,4096]{1,0:T(8,128)(2,1)}, bf16[64,4096]{1,0:T(8,128)(2,1)S(1)}, u32[]{:S(2)}, u32[]{:S(2)}) %collective-permute-start) | collective-permute-done | bytes 524320 | tf_op jit(solution)/shard_map/ppermute | solution.py:250
  14.6 1.5 collective-permute-start.7
  16.6 1.3 copy.11.count_ref
  17.9 1.3 copy.12.dest_ref
  19.9 1.8 %shard_map.104.plan_ref = s32[4,17]{1,0:T(4,128)} custom-call(s32[2]{0:T(128)} %pad_add_fusion.where_ref, s32[4]{0:T(128)} %layers_ref.1, s32[3,2]{1,0:T(4,128)} %copy.11.count_ref, s32[3,2]{1,0:T(4,128)} %copy.12.dest_ref), custom_call_target="tpu_custom_call" | custom-call | tf_op jit(solution)/shard_map/pallas_call | solution.py:82
  22.3 7.3 %collective-permute-done.7.refs_1_ = bf16[64,4096]{1,0:T(8,128)(2,1)S(1)} collective-permute-done((bf16[64,4096]{1,0:T(8,128)(2,1)}, bf16[64,4096]{1,0:T(8,128)(2,1)S(1)}, u32[]{:S(2)}, u32[]{:S(2)}) %collective-permute-start.7) | collective-permute-done | bytes 524320 | tf_op jit(solution)/shard_map/ppermute | solution.py:250
  29.6 9.2 %collective-permute-done.10.refs_5_ = bf16[64,4096]{1,0:T(8,128)(2,1)S(1)} collective-permute-done((bf16[64,4096]{1,0:T(8,128)(2,1)}, bf16[64,4096]{1,0:T(8,128)(2,1)S(1)}, u32[]{:S(2)}, u32[]{:S(2)}) %collective-permute-start.10) | collective-permute-done | bytes 524320 | tf_op jit(solution)/shard_map/ppermute | solution.py:250
  39.7 1.0 copy-done
  42.7 25.3 %shard_map.105 = (bf16[256,4096]{1,0:T(8,128)(2,1)}, bf16[64,4096]{1,0:T(8,128)(2,1)S(1)}) custom-call(s32[4,17]{1,0:T(4,128)S(1)} %copy-done.4, s32[2]{0:T(128)S(1)} %copy-done.5, bf16[64,4096]{1,0:T(8,128)(2,1)S(1)} %bitcast.12, bf16[64,4096]{1,0:T(8,128)(2,1)S(1)} %collective-permute-done.refs_1_, bf16[64,4096]{1,0:T(8,128)(2,1)} %copy-done.9, ...), custom_call_target="tpu_custom_call" | custom-call | flops 9395240960 | bytes 58720256 | tf_op jit(solution)/shard_map/pallas_call | solution.py:221
  70.0 34.4 %shard_map.106 = (bf16[256,4096]{1,0:T(8,128)(2,1)}, bf16[64,4096]{1,0:T(8,128)(2,1)S(1)}, bf16[64,4096]{1,0:T(8,128)(2,1)S(1)}) custom-call(s32[4,17]{1,0:T(4,128)S(1)} %copy-done.4, s32[2]{0:T(128)S(1)} %copy-done.5, bf16[64,4096]{1,0:T(8,128)(2,1)S(1)} %bitcast.15, bf16[64,4096]{1,0:T(8,128)(2,1)} %copy-done.7, bf16[64,4096]{1,0:T(8,128)(2,1)} %copy-done.11, ...), custom_call_target="tpu_custom_call" | custom-call | flops 14092861440 | bytes 58720256 | tf_op jit(solution)/shard_map/pallas_call | solution.py:221
  104.4 1.3 constant_dynamic-slice_fusion.1
  106.2 1.6 constant_dynamic-slice_fusion.4
  108.0 1.5 collective-permute-start.4
  110.0 1.5 add_convert_fusion
  111.6 1.6 collective-permute-start.14
  113.2 8.6 %collective-permute-done.4 = bf16[64,4096]{1,0:T(8,128)(2,1)S(1)} collective-permute-done((bf16[64,4096]{1,0:T(8,128)(2,1)S(1)}, bf16[64,4096]{1,0:T(8,128)(2,1)S(1)}, u32[]{:S(2)}, u32[]{:S(2)}) %collective-permute-start.4) | collective-permute-done | bytes 524320 | tf_op jit(solution)/shard_map/ppermute | solution.py:290
  121.8 12.2 %collective-permute-done.3 = bf16[64,4096]{1,0:T(8,128)(2,1)S(1)} collective-permute-done((bf16[64,4096]{1,0:T(8,128)(2,1)S(1)}, bf16[64,4096]{1,0:T(8,128)(2,1)S(1)}, u32[]{:S(2)}, u32[]{:S(2)}) %collective-permute-start.3) | collective-permute-done | bytes 524320 | tf_op jit(solution)/shard_map/ppermute | solution.py:250
  134.0 1.4 add_convert_fusion.1
  135.3 3.4 %collective-permute-start.6 = (bf16[64,4096]{1,0:T(8,128)(2,1)S(1)}, bf16[64,4096]{1,0:T(8,128)(2,1)S(1)}, u32[]{:S(2)}, u32[]{:S(2)}) collective-permute-start(bf16[64,4096]{1,0:T(8,128)(2,1)S(1)} %add_convert_fusion.1), channel_id=1, source_target_pairs={{0,2},{2,4},{4,6},{6,8},{8,10},{10,12},{12,14},{1,3},{3,5},{5,7},{... | collective-permute-start | bytes 1572872 | tf_op jit(solution)/shard_map/ppermute | solution.py:20
  138.7 6.0 %collective-permute-done.14 = bf16[64,4096]{1,0:T(8,128)(2,1)S(1)} collective-permute-done((bf16[64,4096]{1,0:T(8,128)(2,1)S(1)}, bf16[64,4096]{1,0:T(8,128)(2,1)S(1)}, u32[]{:S(2)}, u32[]{:S(2)}) %collective-permute-start.14) | collective-permute-done | bytes 524320 | tf_op jit(solution)/shard_map/ppermute | solution.py:250
  145.6 3.3 %collective-permute-start.15 = (bf16[64,4096]{1,0:T(8,128)(2,1)S(1)}, bf16[64,4096]{1,0:T(8,128)(2,1)S(1)}, u32[]{:S(2)}, u32[]{:S(2)}) collective-permute-start(bf16[64,4096]{1,0:T(8,128)(2,1)S(1)} %fusion.4), channel_id=1, source_target_pairs={{2,0},{4,2},{6,4},{8,6},{10,8},{12,10},{14,12},{3,1},{5,3},{7,5},{... | collective-permute-start | bytes 1572872 | tf_op jit(solution)/shard_map/ppermute | solution.py:20
  148.9 2.3 %collective-permute-done.6 = bf16[64,4096]{1,0:T(8,128)(2,1)S(1)} collective-permute-done((bf16[64,4096]{1,0:T(8,128)(2,1)S(1)}, bf16[64,4096]{1,0:T(8,128)(2,1)S(1)}, u32[]{:S(2)}, u32[]{:S(2)}) %collective-permute-start.6) | collective-permute-done | bytes 524320 | tf_op jit(solution)/shard_map/ppermute | solution.py:20
  151.2 11.1 %collective-permute-done.15 = bf16[64,4096]{1,0:T(8,128)(2,1)S(1)} collective-permute-done((bf16[64,4096]{1,0:T(8,128)(2,1)S(1)}, bf16[64,4096]{1,0:T(8,128)(2,1)S(1)}, u32[]{:S(2)}, u32[]{:S(2)}) %collective-permute-start.15) | collective-permute-done | bytes 524320 | tf_op jit(solution)/shard_map/ppermute | solution.py:20
  (55 shorter events, 10.2 us)
Async XLA Ops:
  0.6 13.9 %collective-permute-start = (bf16[64,4096]{1,0:T(8,128)(2,1)}, bf16[64,4096]{1,0:T(8,128)(2,1)S(1)}, u32[]{:S(2)}, u32[]{:S(2)}) collective-permute-start(bf16[64,4096]{1,0:T(8,128)(2,1)} %bitcast.10), channel_id=1, source_target_pairs={{0,16},{16,0},{1,17},{17,1},{2,18},{18,2},{3,19},{19,3},{4,20},{20... | collective-permute-start | bytes 1572872 | tf_op jit(solution)/shard_map/ppermute | solution.py:250
  2.2 20.0 %collective-permute-start.1 = (bf16[64,4096]{1,0:T(8,128)(2,1)}, bf16[64,4096]{1,0:T(8,128)(2,1)S(1)}, u32[]{:S(2)}, u32[]{:S(2)}) collective-permute-start(bf16[64,4096]{1,0:T(8,128)(2,1)} %bitcast.11), channel_id=1, source_target_pairs={{0,1},{1,0},{2,3},{3,2},{4,5},{5,4},{6,7},{7,6},{8,9},{9,8},{10,11... | collective-permute-start | bytes 1572872 | tf_op jit(solution)/shard_map/ppermute | solution.py:250
  14.6 15.1 %collective-permute-start.7 = (bf16[64,4096]{1,0:T(8,128)(2,1)}, bf16[64,4096]{1,0:T(8,128)(2,1)S(1)}, u32[]{:S(2)}, u32[]{:S(2)}) collective-permute-start(bf16[64,4096]{1,0:T(8,128)(2,1)} %bitcast.13), channel_id=1, source_target_pairs={{0,16},{16,0},{1,17},{17,1},{2,18},{18,2},{3,19},{19,3},{4,20},{20... | collective-permute-start | bytes 1572872 | tf_op jit(solution)/shard_map/ppermute | solution.py:250
  16.1 22.7 %collective-permute-start.10 = (bf16[64,4096]{1,0:T(8,128)(2,1)}, bf16[64,4096]{1,0:T(8,128)(2,1)S(1)}, u32[]{:S(2)}, u32[]{:S(2)}) collective-permute-start(bf16[64,4096]{1,0:T(8,128)(2,1)} %bitcast.20), channel_id=1, source_target_pairs={{0,16},{16,0},{1,17},{17,1},{2,18},{18,2},{3,19},{19,3},{4,20},{20... | collective-permute-start | bytes 1572872 | tf_op jit(solution)/shard_map/ppermute | solution.py:250
  16.6 22.2 %collective-permute-start.2 = (bf16[64,4096]{1,0:T(8,128)(2,1)S(1)}, bf16[64,4096]{1,0:T(8,128)(2,1)S(1)}, u32[]{:S(2)}, u32[]{:S(2)}) collective-permute-start(bf16[64,4096]{1,0:T(8,128)(2,1)S(1)} %collective-permute-done.refs_1_), channel_id=1, source_target_pairs={{0,1},{1,0},{2,3},{3,2},{4,5},{5,4},{6,7},{7,6},{8,9},{9,8},{10,11... | collective-permute-start | bytes 1572872 | tf_op jit(solution)/shard_map/ppermute | solution.py:250
  21.6 46.4 %collective-permute-start.8 = (bf16[64,4096]{1,0:T(8,128)(2,1)}, bf16[64,4096]{1,0:T(8,128)(2,1)S(1)}, u32[]{:S(2)}, u32[]{:S(2)}) collective-permute-start(bf16[64,4096]{1,0:T(8,128)(2,1)} %bitcast.14), channel_id=1, source_target_pairs={{0,1},{1,0},{2,3},{3,2},{4,5},{5,4},{6,7},{7,6},{8,9},{9,8},{10,11... | collective-permute-start | bytes 1572872 | tf_op jit(solution)/shard_map/ppermute | solution.py:250
  22.2 17.4 %copy-start.9 = (bf16[64,4096]{1,0:T(8,128)(2,1)}, bf16[64,4096]{1,0:T(8,128)(2,1)S(1)}, u32[]{:S(2)}) copy-start(bf16[64,4096]{1,0:T(8,128)(2,1)S(1)} %collective-permute-done.1.refs_2_) | copy-start | bytes 1572868
  22.2 45.9 %collective-permute-start.11 = (bf16[64,4096]{1,0:T(8,128)(2,1)}, bf16[64,4096]{1,0:T(8,128)(2,1)S(1)}, u32[]{:S(2)}, u32[]{:S(2)}) collective-permute-start(bf16[64,4096]{1,0:T(8,128)(2,1)} %bitcast.21), channel_id=1, source_target_pairs={{0,1},{1,0},{2,3},{3,2},{4,5},{5,4},{6,7},{7,6},{8,9},{9,8},{10,11... | collective-permute-start | bytes 1572872 | tf_op jit(solution)/shard_map/ppermute | solution.py:250
  29.6 38.4 %copy-start.7 = (bf16[64,4096]{1,0:T(8,128)(2,1)}, bf16[64,4096]{1,0:T(8,128)(2,1)S(1)}, u32[]{:S(2)}) copy-start(bf16[64,4096]{1,0:T(8,128)(2,1)S(1)} %collective-permute-done.7.refs_1_) | copy-start | bytes 1572868
  29.6 38.5 %collective-permute-start.9 = (bf16[64,4096]{1,0:T(8,128)(2,1)S(1)}, bf16[64,4096]{1,0:T(8,128)(2,1)S(1)}, u32[]{:S(2)}, u32[]{:S(2)}) collective-permute-start(bf16[64,4096]{1,0:T(8,128)(2,1)S(1)} %collective-permute-done.7.refs_1_), channel_id=1, source_target_pairs={{0,1},{1,0},{2,3},{3,2},{4,5},{5,4},{6,7},{7,6},{8,9},{9,8},{10,11... | collective-permute-start | bytes 1572872 | tf_op jit(solution)/shard_map/ppermute | solution.py:250
  38.8 29.3 %copy-start.8 = (bf16[64,4096]{1,0:T(8,128)(2,1)}, bf16[64,4096]{1,0:T(8,128)(2,1)S(1)}, u32[]{:S(2)}) copy-start(bf16[64,4096]{1,0:T(8,128)(2,1)S(1)} %collective-permute-done.10.refs_5_) | copy-start | bytes 1572868
  38.8 29.3 %collective-permute-start.12 = (bf16[64,4096]{1,0:T(8,128)(2,1)S(1)}, bf16[64,4096]{1,0:T(8,128)(2,1)S(1)}, u32[]{:S(2)}, u32[]{:S(2)}) collective-permute-start(bf16[64,4096]{1,0:T(8,128)(2,1)S(1)} %collective-permute-done.10.refs_5_), channel_id=1, source_target_pairs={{0,1},{1,0},{2,3},{3,2},{4,5},{5,4},{6,7},{7,6},{8,9},{9,8},{10,11... | collective-permute-start | bytes 1572872 | tf_op jit(solution)/shard_map/ppermute | solution.py:250
  39.7 1.0 copy-start
  42.7 27.3 %copy-start.1 = (bf16[1,1,64,4096]{3,2,1,0:T(8,128)(2,1)S(1)}, bf16[1,1,64,4096]{3,2,1,0:T(8,128)(2,1)}, u32[]{:S(2)}) copy-start(bf16[1,1,64,4096]{3,2,1,0:T(8,128)(2,1)} %param.10) | copy-start | bytes 1572868
  42.7 27.3 %copy-start.3 = (bf16[1,4096]{1,0:T(2,128)(2,1)S(1)}, bf16[1,4096]{1,0:T(2,128)(2,1)}, u32[]{:S(2)}) copy-start(bf16[1,4096]{1,0:T(2,128)(2,1)} %refs_8_.1) | copy-start | bytes 24580
  68.1 1.1 copy-start.13
  105.7 4.3 %collective-permute-start.13 = (bf16[128,4096]{1,0:T(8,128)(2,1)S(1)}, bf16[128,4096]{1,0:T(8,128)(2,1)}, u32[]{:S(2)}, u32[]{:S(2)}) collective-permute-start(bf16[128,4096]{1,0:T(8,128)(2,1)S(1)} %constant_dynamic-slice_fusion.1), channel_id=1, source_target_pairs={{0,1},{1,0},{2,3},{3,2},{4,5},{5,4},{6,7},{7,6},{8,9},{9,8},{10,11... | collective-permute-start | bytes 3145736 | tf_op jit(solution)/shard_map/ppermute | solution.py:250
  106.2 3.8 %copy-start.6 = (bf16[256,4096]{1,0:T(8,128)(2,1)S(1)}, bf16[256,4096]{1,0:T(8,128)(2,1)}, u32[]{:S(2)}) copy-start(bf16[256,4096]{1,0:T(8,128)(2,1)} %get-tuple-element.21) | copy-start | bytes 6291460
  107.8 5.3 %collective-permute-start.5 = (bf16[64,4096]{1,0:T(8,128)(2,1)S(1)}, bf16[64,4096]{1,0:T(8,128)(2,1)S(1)}, u32[]{:S(2)}, u32[]{:S(2)}) collective-permute-start(bf16[64,4096]{1,0:T(8,128)(2,1)S(1)} %get-tuple-element.25), channel_id=1, source_target_pairs={{0,1},{1,0},{2,3},{3,2},{4,5},{5,4},{6,7},{7,6},{8,9},{9,8},{10,11... | collective-permute-start | bytes 1572872 | tf_op jit(solution)/shard_map/ppermute | solution.py:250
  108.0 13.8 %collective-permute-start.4 = (bf16[64,4096]{1,0:T(8,128)(2,1)S(1)}, bf16[64,4096]{1,0:T(8,128)(2,1)S(1)}, u32[]{:S(2)}, u32[]{:S(2)}) collective-permute-start(bf16[64,4096]{1,0:T(8,128)(2,1)S(1)} %get-tuple-element.26), channel_id=1, source_target_pairs={{0,17},{1,16},{16,1},{17,0},{2,19},{3,18},{18,3},{19,2},{4,21},{5,... | collective-permute-start | bytes 1572872 | tf_op jit(solution)/shard_map/ppermute | solution.py:290
  109.5 24.4 %collective-permute-start.3 = (bf16[64,4096]{1,0:T(8,128)(2,1)S(1)}, bf16[64,4096]{1,0:T(8,128)(2,1)S(1)}, u32[]{:S(2)}, u32[]{:S(2)}) collective-permute-start(bf16[64,4096]{1,0:T(8,128)(2,1)S(1)} %get-tuple-element.24), channel_id=1, source_target_pairs={{0,16},{16,0},{1,17},{17,1},{2,18},{18,2},{3,19},{19,3},{4,20},{20... | collective-permute-start | bytes 1572872 | tf_op jit(solution)/shard_map/ppermute | solution.py:250
  111.6 33.2 %collective-permute-start.14 = (bf16[64,4096]{1,0:T(8,128)(2,1)S(1)}, bf16[64,4096]{1,0:T(8,128)(2,1)S(1)}, u32[]{:S(2)}, u32[]{:S(2)}) collective-permute-start(bf16[64,4096]{1,0:T(8,128)(2,1)S(1)} %constant_dynamic-slice_fusion), channel_id=1, source_target_pairs={{0,16},{16,0},{1,17},{17,1},{2,18},{18,2},{3,19},{19,3},{4,20},{20... | collective-permute-start | bytes 1572872 | tf_op jit(solution)/shard_map/ppermute | solution.py:250
  135.3 15.9 %collective-permute-start.6 = (bf16[64,4096]{1,0:T(8,128)(2,1)S(1)}, bf16[64,4096]{1,0:T(8,128)(2,1)S(1)}, u32[]{:S(2)}, u32[]{:S(2)}) collective-permute-start(bf16[64,4096]{1,0:T(8,128)(2,1)S(1)} %add_convert_fusion.1), channel_id=1, source_target_pairs={{0,2},{2,4},{4,6},{6,8},{8,10},{10,12},{12,14},{1,3},{3,5},{5,7},{... | collective-permute-start | bytes 1572872 | tf_op jit(solution)/shard_map/ppermute | solution.py:20
  145.6 16.8 %collective-permute-start.15 = (bf16[64,4096]{1,0:T(8,128)(2,1)S(1)}, bf16[64,4096]{1,0:T(8,128)(2,1)S(1)}, u32[]{:S(2)}, u32[]{:S(2)}) collective-permute-start(bf16[64,4096]{1,0:T(8,128)(2,1)S(1)} %fusion.4), channel_id=1, source_target_pairs={{2,0},{4,2},{6,4},{8,6},{10,8},{12,10},{14,12},{3,1},{5,3},{7,5},{... | collective-permute-start | bytes 1572872 | tf_op jit(solution)/shard_map/ppermute | solution.py:20
  (7 other events, 5.4 us)

commit v3 on v2

--- a/solution.py
+++ b/solution.py
@@ -268,29 +268,21 @@
     return lax.dynamic_slice_in_dim(block, index * rows, rows)
 
 
-def scatter(partial):
-    if in_pairs():
-        for axis in ("tp", "rep"):
-            index = lax.axis_index(axis)
-            arrived = other(half(partial, 1 - index), axis)
-            partial = half(partial, index).astype(jnp.float32) + arrived.astype(jnp.float32)
-            if axis == "tp":
-                partial = partial.astype(jnp.bfloat16)
-        return partial
-    near = lax.psum_scatter(partial, "tp", scatter_dimension=0, tiled=True)
+def scatter_near(partial):
+    if in_pairs():
+        index = lax.axis_index("tp")
+        arrived = other(half(partial, 1 - index), "tp")
+        near = half(partial, index).astype(jnp.float32) + arrived.astype(jnp.float32)
+        return near.astype(jnp.bfloat16)
+    return lax.psum_scatter(partial, "tp", scatter_dimension=0, tiled=True)
+
+
+def scatter_far(near):
+    if in_pairs():
+        index = lax.axis_index("rep")
+        arrived = other(half(near, 1 - index), "rep")
+        return half(near, index).astype(jnp.float32) + arrived.astype(jnp.float32)
     return lax.psum_scatter(near, "rep", scatter_dimension=0, tiled=True).astype(jnp.float32)
-
-
-def scatter_direct(partial, shard, shard_rows):
-    if not in_pairs():
-        return scatter(partial), []
-    piece = lambda k: lax.dynamic_slice_in_dim(partial, lax.bitwise_xor(shard, k) * shard_rows, shard_rows)
-    arrived = [
-        other(piece(1), "rep"),
-        lax.ppermute(piece(3), ("rep", "tp"), [(i, 3 - i) for i in range(4)]),
-        other(piece(2), "tp"),
-    ]
-    return piece(0).astype(jnp.float32), arrived
 
 
 def local(
@@ -319,21 +311,25 @@
             (other(fresh_own, "rep"), saved_own, grad_own)
         )
     fresh = gather(fresh_own, fresh_across)
-    saved, upstream = gather(saved_own), gather(grad_own)
+    saved_across = grad_across = None
+    if in_pairs():
+        saved_across, grad_across = other(saved_own, "rep"), other(grad_own, "rep")
     mixed, mine_fresh = run_layer(
         forward_kernel, plan, where, [fresh], norm_gain, w_up, w_down, blocks, shard_rows, 2
     )
-    mixed, plan = lax.optimization_barrier((mixed, plan))
-    total, arrived = scatter_direct(mixed, shard, shard_rows)
+    if in_pairs():
+        mixed, saved_across, grad_across = lax.optimization_barrier(
+            (mixed, saved_across, grad_across)
+        )
+    saved, upstream = gather(saved_own, saved_across), gather(grad_own, grad_across)
+    near, plan = lax.optimization_barrier((scatter_near(mixed), plan))
     returned, mine_saved, mine_grad = run_layer(
         backward_kernel, plan, where, [saved, upstream], norm_gain, w_up, w_down, blocks, shard_rows, 3
     )
-    for block in arrived:
-        total = total + block.astype(jnp.float32)
-    result = (mine_fresh.astype(jnp.float32) + total).astype(jnp.bfloat16)
+    result = (mine_fresh.astype(jnp.float32) + scatter_far(near)).astype(jnp.bfloat16)
     arrive_forward = from_behind(result, "pipe", 1)
     gradient = (
-        mine_grad.astype(jnp.float32) + norm_back(mine_saved, norm_gain, scatter(returned))
+        mine_grad.astype(jnp.float32) + norm_back(mine_saved, norm_gain, scatter_far(scatter_near(returned)))
     ).astype(jnp.bfloat16)
     arrive_backward = from_behind(gradient, "pipe", -1)
     return (arrive_forward[None, None], arrive_backward[None, None])

time: 165 us -> 142 us (0.86)
  waiting for transfers between devices: 69.1 us -> 44.5 us
    ppermute x13, waiting for transfers between devices: 47 us -> 32.2 us  [other(): return lax.ppermute(block, axis, [(0, 1), (1, 0)])]
    ppermute x1 -> x0, waiting for transfers between devices: 8.62 us -> none  [scatter_direct(): lax.ppermute(piece(3), ('rep', 'tp'), [(i, 3 - i) for i in range(4)])]
    dynamic_slice x2 -> x4, local copies, waits for them, and re-layouts: 1.35 us -> 3.72 us  [half(): return lax.dynamic_slice_in_dim(block, index * rows, rows)]
    convert_element_type x2 -> x3, other arithmetic: 2.85 us -> 3.77 us  [the longest x2 3.57 us: scatter_near(): return near.astype(jnp.bfloat16)]
    unnamed x34 -> x32, local copies, waits for them, and re-layouts: 10.1 us -> 9.53 us
  transfers between devices with their start and end apart: 16 -> 15, of which waited for: 8 -> 8; matrix products, arithmetic and copies ran while one was open for 5% -> 6% of each run, Pallas kernels for 17% -> 19%
where the time goes in v3:
time: 142 us; the launch traced here: 140 us
  Pallas kernels  61.5 us (43%)
  waiting for transfers between devices  44.5 us (31%)
  starting transfers between devices  14.8 us (10%)
  local copies, waits for them, and re-layouts  13.2 us (9%)
  other arithmetic  5.27 us (4%)
    pallas_call x2, Pallas kernels, run_layer(): pl.pallas_call(functools.partial(kernel, blocks, shard_rows // BLOCK, par...  59.7 us
    ppermute x13, waiting for transfers between devices, other(): return lax.ppermute(block, axis, [(0, 1), (1, 0)])  32.2 us
    ppermute x2, waiting for transfers between devices, from_behind(): return lax.ppermute(block, axis, route)  12.3 us
    unnamed x32, local copies, waits for them, and re-layouts  9.53 us
    ppermute x13, starting transfers between devices, other(): return lax.ppermute(block, axis, [(0, 1), (1, 0)])  8.13 us
    ppermute x2, starting transfers between devices, from_behind(): return lax.ppermute(block, axis, route)  6.67 us
    dynamic_slice x4, local copies, waits for them, and re-layouts, half(): return lax.dynamic_slice_in_dim(block, index * rows, rows)  3.72 us
    convert_element_type x2, other arithmetic, scatter_near(): return near.astype(jnp.bfloat16)  3.57 us
  transfers between devices with their start and end apart: 15, of which 8 were waited for; matrix products, arithmetic and copies ran while one was open for 6% of the time, Pallas kernels for 19%

profile of v3, /device:TPU:8, one launch (start us, length us, event | category | flops | bytes accessed | tf_op | source)
XLA Modules:
  0.0 140.1 jit_solution(10623698536457971786)
XLA Ops:
  0.6 1.6 %collective-permute-start = (bf16[64,4096]{1,0:T(8,128)(2,1)}, bf16[64,4096]{1,0:T(8,128)(2,1)S(1)}, u32[]{:S(2)}, u32[]{:S(2)}) collective-permute-start(bf16[64,4096]{1,0:T(8,128)(2,1)} %bitcast.10), channel_id=1, source_target_pairs={{0,16},{16,0},{1,17},{17,1},{2,18},{18,2},{3,19},{19,3},{4,20},{20... | collective-permute-start | bytes 1572872 | tf_op jit(solution)/shard_map/ppermute | solution.py:250
  2.2 12.4 %collective-permute-done.refs_1_ = bf16[64,4096]{1,0:T(8,128)(2,1)S(1)} collective-permute-done((bf16[64,4096]{1,0:T(8,128)(2,1)}, bf16[64,4096]{1,0:T(8,128)(2,1)S(1)}, u32[]{:S(2)}, u32[]{:S(2)}) %collective-permute-start) | collective-permute-done | bytes 524320 | tf_op jit(solution)/shard_map/ppermute | solution.py:250
  14.6 1.3 copy.11.count_ref
  15.9 1.3 copy.12.dest_ref
  17.8 1.8 %shard_map.104.plan_ref = s32[4,17]{1,0:T(4,128)} custom-call(s32[2]{0:T(128)} %pad_add_fusion.where_ref, s32[4]{0:T(128)} %layers_ref.1, s32[3,2]{1,0:T(4,128)} %copy.11.count_ref, s32[3,2]{1,0:T(4,128)} %copy.12.dest_ref), custom_call_target="tpu_custom_call" | custom-call | tf_op jit(solution)/shard_map/pallas_call | solution.py:82
  19.6 1.6 %collective-permute-start.3 = (bf16[64,4096]{1,0:T(8,128)(2,1)}, bf16[64,4096]{1,0:T(8,128)(2,1)}, u32[]{:S(2)}, u32[]{:S(2)}) collective-permute-start(bf16[64,4096]{1,0:T(8,128)(2,1)} %bitcast.13), channel_id=1, source_target_pairs={{0,16},{16,0},{1,17},{17,1},{2,18},{18,2},{3,19},{19,3},{4,20},{20... | collective-permute-start | bytes 1572872 | tf_op jit(solution)/shard_map/ppermute | solution.py:250
  22.7 1.0 copy-done
  25.7 25.3 %shard_map.105 = (bf16[256,4096]{1,0:T(8,128)(2,1)}, bf16[64,4096]{1,0:T(8,128)(2,1)S(1)}) custom-call(s32[4,17]{1,0:T(4,128)S(1)} %copy-done.4, s32[2]{0:T(128)S(1)} %copy-done.6, bf16[64,4096]{1,0:T(8,128)(2,1)S(1)} %bitcast.12, bf16[64,4096]{1,0:T(8,128)(2,1)S(1)} %collective-permute-done.refs_1_, bf16[64,4096]{1,0:T(8,128)(2,1)} %copy-done.8, ...), custom_call_target="tpu_custom_call" | custom-call | flops 9395240960 | bytes 58720256 | tf_op jit(solution)/shard_map/pallas_call | solution.py:221
  51.0 1.4 constant_dynamic-slice_fusion.3
  53.6 2.3 %collective-permute-done.5 = bf16[128,4096]{1,0:T(8,128)(2,1)} collective-permute-done((bf16[128,4096]{1,0:T(8,128)(2,1)S(1)}, bf16[128,4096]{1,0:T(8,128)(2,1)}, u32[]{:S(2)}, u32[]{:S(2)}) %collective-permute-start.5) | collective-permute-done | bytes 1048608 | tf_op jit(solution)/shard_map/ppermute | solution.py:250
  55.9 1.8 %add_convert_fusion.1 = bf16[128,4096]{1,0:T(8,128)(2,1)S(1)} fusion(bf16[128,4096]{1,0:T(8,128)(2,1)} %collective-permute-done.5, bf16[256,4096]{1,0:T(8,128)(2,1)} %get-tuple-element.20, s32[]{:T(128)S(6)} %select_n.16), kind=kLoop, calls=%fused_computation.1 | loop fusion | flops 2097152 | bytes 3145732 | tf_op jit(solution)/shard_map/convert_element_type | solution.py:276
  59.6 34.4 %shard_map.106 = (bf16[256,4096]{1,0:T(8,128)(2,1)}, bf16[64,4096]{1,0:T(8,128)(2,1)S(1)}, bf16[64,4096]{1,0:T(8,128)(2,1)S(1)}) custom-call(s32[4,17]{1,0:T(4,128)S(1)} %copy-done.5, s32[2]{0:T(128)S(1)} %copy-done.7, bf16[64,4096]{1,0:T(8,128)(2,1)S(1)} %bitcast.15, bf16[64,4096]{1,0:T(8,128)(2,1)} %collective-permute-done.3.refs_1_, ...), custom_call_target="tpu_custom_call" | custom-call | flops 14092861440 | bytes 58720256 | tf_op jit(solution)/shard_map/pallas_call | solution.py:221
  94.1 2.3 %constant_dynamic-slice_fusion.1 = bf16[128,4096]{1,0:T(8,128)(2,1)} fusion(bf16[256,4096]{1,0:T(8,128)(2,1)} %get-tuple-element.27, s32[]{:T(128)S(6)} %select_n.17), kind=kLoop, calls=%fused_computation.14 | loop fusion | bytes 2097156 | tf_op jit(solution)/shard_map/dynamic_slice | solution.py:268
  96.5 1.6 %collective-permute-start.6 = (bf16[64,4096]{1,0:T(8,128)(2,1)S(1)}, bf16[64,4096]{1,0:T(8,128)(2,1)S(1)}, u32[]{:S(2)}, u32[]{:S(2)}) collective-permute-start(bf16[64,4096]{1,0:T(8,128)(2,1)S(1)} %constant_dynamic-slice_fusion.2), channel_id=1, source_target_pairs={{0,16},{16,0},{1,17},{17,1},{2,18},{18,2},{3,19},{19,3},{4,20},{20... | collective-permute-start | bytes 1572872 | tf_op jit(solution)/shard_map/ppermute | solution.py:250
  98.1 1.2 collective-permute-done.12
  99.3 1.8 %add_convert_fusion = bf16[128,4096]{1,0:T(8,128)(2,1)S(1)} fusion(bf16[128,4096]{1,0:T(8,128)(2,1)} %collective-permute-done.12, bf16[256,4096]{1,0:T(8,128)(2,1)} %get-tuple-element.27, s32[]{:T(128)S(6)} %select_n.16), kind=kLoop, calls=%fused_computation | loop fusion | flops 2097152 | bytes 3145732 | tf_op jit(solution)/shard_map/convert_element_type | solution.py:276
  101.2 1.6 %collective-permute-start.13 = (bf16[64,4096]{1,0:T(8,128)(2,1)S(1)}, bf16[64,4096]{1,0:T(8,128)(2,1)S(1)}, u32[]{:S(2)}, u32[]{:S(2)}) collective-permute-start(bf16[64,4096]{1,0:T(8,128)(2,1)S(1)} %constant_dynamic-slice_fusion), channel_id=1, source_target_pairs={{0,16},{16,0},{1,17},{17,1},{2,18},{18,2},{3,19},{19,3},{4,20},{20... | collective-permute-start | bytes 1572872 | tf_op jit(solution)/shard_map/ppermute | solution.py:250
  102.8 8.5 %collective-permute-done.6 = bf16[64,4096]{1,0:T(8,128)(2,1)S(1)} collective-permute-done((bf16[64,4096]{1,0:T(8,128)(2,1)S(1)}, bf16[64,4096]{1,0:T(8,128)(2,1)S(1)}, u32[]{:S(2)}, u32[]{:S(2)}) %collective-permute-start.6) | collective-permute-done | bytes 524320 | tf_op jit(solution)/shard_map/ppermute | solution.py:250
  111.5 3.4 %collective-permute-start.7 = (bf16[64,4096]{1,0:T(8,128)(2,1)S(1)}, bf16[64,4096]{1,0:T(8,128)(2,1)S(1)}, u32[]{:S(2)}, u32[]{:S(2)}) collective-permute-start(bf16[64,4096]{1,0:T(8,128)(2,1)S(1)} %add_convert_fusion.2), channel_id=1, source_target_pairs={{0,2},{2,4},{4,6},{6,8},{8,10},{10,12},{12,14},{1,3},{3,5},{5,7},{... | collective-permute-start | bytes 1572872 | tf_op jit(solution)/shard_map/ppermute | solution.py:20
  114.9 7.2 %collective-permute-done.13 = bf16[64,4096]{1,0:T(8,128)(2,1)S(1)} collective-permute-done((bf16[64,4096]{1,0:T(8,128)(2,1)S(1)}, bf16[64,4096]{1,0:T(8,128)(2,1)S(1)}, u32[]{:S(2)}, u32[]{:S(2)}) %collective-permute-start.13) | collective-permute-done | bytes 524320 | tf_op jit(solution)/shard_map/ppermute | solution.py:250
  122.9 3.3 %collective-permute-start.14 = (bf16[64,4096]{1,0:T(8,128)(2,1)S(1)}, bf16[64,4096]{1,0:T(8,128)(2,1)S(1)}, u32[]{:S(2)}, u32[]{:S(2)}) collective-permute-start(bf16[64,4096]{1,0:T(8,128)(2,1)S(1)} %fusion.4), channel_id=1, source_target_pairs={{2,0},{4,2},{6,4},{8,6},{10,8},{12,10},{14,12},{3,1},{5,3},{7,5},{... | collective-permute-start | bytes 1572872 | tf_op jit(solution)/shard_map/ppermute | solution.py:20
  126.2 1.1 collective-permute-done.7
  127.3 11.2 %collective-permute-done.14 = bf16[64,4096]{1,0:T(8,128)(2,1)S(1)} collective-permute-done((bf16[64,4096]{1,0:T(8,128)(2,1)S(1)}, bf16[64,4096]{1,0:T(8,128)(2,1)S(1)}, u32[]{:S(2)}, u32[]{:S(2)}) %collective-permute-start.14) | collective-permute-done | bytes 524320 | tf_op jit(solution)/shard_map/ppermute | solution.py:20
  138.5 0.8 copy.15
  (53 shorter events, 9.2 us)
Async XLA Ops:
  0.6 13.9 %collective-permute-start = (bf16[64,4096]{1,0:T(8,128)(2,1)}, bf16[64,4096]{1,0:T(8,128)(2,1)S(1)}, u32[]{:S(2)}, u32[]{:S(2)}) collective-permute-start(bf16[64,4096]{1,0:T(8,128)(2,1)} %bitcast.10), channel_id=1, source_target_pairs={{0,16},{16,0},{1,17},{17,1},{2,18},{18,2},{3,19},{19,3},{4,20},{20... | collective-permute-start | bytes 1572872 | tf_op jit(solution)/shard_map/ppermute | solution.py:250
  2.2 19.5 %collective-permute-start.1 = (bf16[64,4096]{1,0:T(8,128)(2,1)}, bf16[64,4096]{1,0:T(8,128)(2,1)S(1)}, u32[]{:S(2)}, u32[]{:S(2)}) collective-permute-start(bf16[64,4096]{1,0:T(8,128)(2,1)} %bitcast.11), channel_id=1, source_target_pairs={{0,1},{1,0},{2,3},{3,2},{4,5},{5,4},{6,7},{7,6},{8,9},{9,8},{10,11... | collective-permute-start | bytes 1572872 | tf_op jit(solution)/shard_map/ppermute | solution.py:250
  14.6 7.1 %collective-permute-start.2 = (bf16[64,4096]{1,0:T(8,128)(2,1)S(1)}, bf16[64,4096]{1,0:T(8,128)(2,1)S(1)}, u32[]{:S(2)}, u32[]{:S(2)}) collective-permute-start(bf16[64,4096]{1,0:T(8,128)(2,1)S(1)} %collective-permute-done.refs_1_), channel_id=1, source_target_pairs={{0,1},{1,0},{2,3},{3,2},{4,5},{5,4},{6,7},{7,6},{8,9},{9,8},{10,11... | collective-permute-start | bytes 1572872 | tf_op jit(solution)/shard_map/ppermute | solution.py:250
  19.6 31.4 %collective-permute-start.3 = (bf16[64,4096]{1,0:T(8,128)(2,1)}, bf16[64,4096]{1,0:T(8,128)(2,1)}, u32[]{:S(2)}, u32[]{:S(2)}) collective-permute-start(bf16[64,4096]{1,0:T(8,128)(2,1)} %bitcast.13), channel_id=1, source_target_pairs={{0,16},{16,0},{1,17},{17,1},{2,18},{18,2},{3,19},{19,3},{4,20},{20... | collective-permute-start | bytes 1572872 | tf_op jit(solution)/shard_map/ppermute | solution.py:250
  21.2 29.8 %collective-permute-start.4 = (bf16[64,4096]{1,0:T(8,128)(2,1)}, bf16[64,4096]{1,0:T(8,128)(2,1)}, u32[]{:S(2)}, u32[]{:S(2)}) collective-permute-start(bf16[64,4096]{1,0:T(8,128)(2,1)} %bitcast.4.refs_4_), channel_id=1, source_target_pairs={{0,16},{16,0},{1,17},{17,1},{2,18},{18,2},{3,19},{19,3},{4,20},{20... | collective-permute-start | bytes 1572872 | tf_op jit(solution)/shard_map/ppermute | solution.py:250
  21.7 1.0 copy-start.9
  22.7 1.0 copy-start
  51.0 1.5 %copy-start.1 = (bf16[1,1,64,4096]{3,2,1,0:T(8,128)(2,1)S(1)}, bf16[1,1,64,4096]{3,2,1,0:T(8,128)(2,1)}, u32[]{:S(2)}) copy-start(bf16[1,1,64,4096]{3,2,1,0:T(8,128)(2,1)} %param.10) | copy-start | bytes 1572868
  52.4 7.2 %copy-start.3 = (bf16[1,4096]{1,0:T(2,128)(2,1)S(1)}, bf16[1,4096]{1,0:T(2,128)(2,1)}, u32[]{:S(2)}) copy-start(bf16[1,4096]{1,0:T(2,128)(2,1)} %refs_8_.1) | copy-start | bytes 24580
  52.4 7.2 %copy-start.5 = (s32[4,17]{1,0:T(4,128)S(1)}, s32[4,17]{1,0:T(4,128)}, u32[]{:S(2)}) copy-start(s32[4,17]{1,0:T(4,128)} %shard_map.104.plan_ref) | copy-start | bytes 820
  52.4 7.2 %copy-start.7 = (s32[2]{0:T(128)S(1)}, s32[2]{0:T(128)}, u32[]{:S(2)}) copy-start(s32[2]{0:T(128)} %pad_add_fusion.where_ref) | copy-start | bytes 28
  52.4 3.5 %collective-permute-start.5 = (bf16[128,4096]{1,0:T(8,128)(2,1)S(1)}, bf16[128,4096]{1,0:T(8,128)(2,1)}, u32[]{:S(2)}, u32[]{:S(2)}) collective-permute-start(bf16[128,4096]{1,0:T(8,128)(2,1)S(1)} %constant_dynamic-slice_fusion.3), channel_id=1, source_target_pairs={{0,1},{1,0},{2,3},{3,2},{4,5},{5,4},{6,7},{7,6},{8,9},{9,8},{10,11... | collective-permute-start | bytes 3145736 | tf_op jit(solution)/shard_map/ppermute | solution.py:250
  52.5 5.2 %collective-permute-start.8 = (bf16[64,4096]{1,0:T(8,128)(2,1)S(1)}, bf16[64,4096]{1,0:T(8,128)(2,1)S(1)}, u32[]{:S(2)}, u32[]{:S(2)}) collective-permute-start(bf16[64,4096]{1,0:T(8,128)(2,1)S(1)} %bitcast.14), channel_id=1, source_target_pairs={{0,1},{1,0},{2,3},{3,2},{4,5},{5,4},{6,7},{7,6},{8,9},{9,8},{10,11... | collective-permute-start | bytes 1572872 | tf_op jit(solution)/shard_map/ppermute | solution.py:250
  53.0 4.7 %collective-permute-start.10 = (bf16[64,4096]{1,0:T(8,128)(2,1)}, bf16[64,4096]{1,0:T(8,128)(2,1)S(1)}, u32[]{:S(2)}, u32[]{:S(2)}) collective-permute-start(bf16[64,4096]{1,0:T(8,128)(2,1)} %bitcast.4.refs_4_), channel_id=1, source_target_pairs={{0,1},{1,0},{2,3},{3,2},{4,5},{5,4},{6,7},{7,6},{8,9},{9,8},{10,11... | collective-permute-start | bytes 1572872 | tf_op jit(solution)/shard_map/ppermute | solution.py:250
  53.1 4.6 %collective-permute-start.9 = (bf16[64,4096]{1,0:T(8,128)(2,1)}, bf16[64,4096]{1,0:T(8,128)(2,1)S(1)}, u32[]{:S(2)}, u32[]{:S(2)}) collective-permute-start(bf16[64,4096]{1,0:T(8,128)(2,1)} %collective-permute-done.3.refs_1_), channel_id=1, source_target_pairs={{0,1},{1,0},{2,3},{3,2},{4,5},{5,4},{6,7},{7,6},{8,9},{9,8},{10,11... | collective-permute-start | bytes 1572872 | tf_op jit(solution)/shard_map/ppermute | solution.py:250
  53.5 4.8 %collective-permute-start.11 = (bf16[64,4096]{1,0:T(8,128)(2,1)}, bf16[64,4096]{1,0:T(8,128)(2,1)S(1)}, u32[]{:S(2)}, u32[]{:S(2)}) collective-permute-start(bf16[64,4096]{1,0:T(8,128)(2,1)} %collective-permute-done.4.refs_5_), channel_id=1, source_target_pairs={{0,1},{1,0},{2,3},{3,2},{4,5},{5,4},{6,7},{7,6},{8,9},{9,8},{10,11... | collective-permute-start | bytes 1572872 | tf_op jit(solution)/shard_map/ppermute | solution.py:250
  57.7 0.8 copy-start.10
  57.7 1.0 copy-start.11
  57.7 1.1 copy-start.12
  96.3 3.0 %collective-permute-start.12 = (bf16[128,4096]{1,0:T(8,128)(2,1)}, bf16[128,4096]{1,0:T(8,128)(2,1)}, u32[]{:S(2)}, u32[]{:S(2)}) collective-permute-start(bf16[128,4096]{1,0:T(8,128)(2,1)} %constant_dynamic-slice_fusion.1), channel_id=1, source_target_pairs={{0,1},{1,0},{2,3},{3,2},{4,5},{5,4},{6,7},{7,6},{8,9},{9,8},{10,11... | collective-permute-start | bytes 3145736 | tf_op jit(solution)/shard_map/ppermute | solution.py:250
  96.5 14.8 %collective-permute-start.6 = (bf16[64,4096]{1,0:T(8,128)(2,1)S(1)}, bf16[64,4096]{1,0:T(8,128)(2,1)S(1)}, u32[]{:S(2)}, u32[]{:S(2)}) collective-permute-start(bf16[64,4096]{1,0:T(8,128)(2,1)S(1)} %constant_dynamic-slice_fusion.2), channel_id=1, source_target_pairs={{0,16},{16,0},{1,17},{17,1},{2,18},{18,2},{3,19},{19,3},{4,20},{20... | collective-permute-start | bytes 1572872 | tf_op jit(solution)/shard_map/ppermute | solution.py:250
  101.2 20.9 %collective-permute-start.13 = (bf16[64,4096]{1,0:T(8,128)(2,1)S(1)}, bf16[64,4096]{1,0:T(8,128)(2,1)S(1)}, u32[]{:S(2)}, u32[]{:S(2)}) collective-permute-start(bf16[64,4096]{1,0:T(8,128)(2,1)S(1)} %constant_dynamic-slice_fusion), channel_id=1, source_target_pairs={{0,16},{16,0},{1,17},{17,1},{2,18},{18,2},{3,19},{19,3},{4,20},{20... | collective-permute-start | bytes 1572872 | tf_op jit(solution)/shard_map/ppermute | solution.py:250
  111.5 15.8 %collective-permute-start.7 = (bf16[64,4096]{1,0:T(8,128)(2,1)S(1)}, bf16[64,4096]{1,0:T(8,128)(2,1)S(1)}, u32[]{:S(2)}, u32[]{:S(2)}) collective-permute-start(bf16[64,4096]{1,0:T(8,128)(2,1)S(1)} %add_convert_fusion.2), channel_id=1, source_target_pairs={{0,2},{2,4},{4,6},{6,8},{8,10},{10,12},{12,14},{1,3},{3,5},{5,7},{... | collective-permute-start | bytes 1572872 | tf_op jit(solution)/shard_map/ppermute | solution.py:20
  122.9 15.6 %collective-permute-start.14 = (bf16[64,4096]{1,0:T(8,128)(2,1)S(1)}, bf16[64,4096]{1,0:T(8,128)(2,1)S(1)}, u32[]{:S(2)}, u32[]{:S(2)}) collective-permute-start(bf16[64,4096]{1,0:T(8,128)(2,1)S(1)} %fusion.4), channel_id=1, source_target_pairs={{2,0},{4,2},{6,4},{8,6},{10,8},{12,10},{14,12},{3,1},{5,3},{7,5},{... | collective-permute-start | bytes 1572872 | tf_op jit(solution)/shard_map/ppermute | solution.py:20
  (5 other events, 3.6 us)
